TPU v7x, 256 devices: a whole 4x4x8 slice. The times are simulated.
256 devices in a mesh: seq: 8 (over y, core), expert: 32 (over z, x).
Axes of the slice: x: 4, y: 4, z: 8, core: 2. Of those that a mesh axis runs over, the one named last changes fastest.
Arguments:
- latents: bfloat16 [32768, 1536], P(('seq', 'expert')), may hold values from -6 to 6
- control: bfloat16 [32768, 1536], P(('seq', 'expert')), may hold values from -6 to 6
- control_scale: float32 [1536], replicated, may hold values from 0.1 to 1.5
- norm_gain: float32 [1536], replicated, may hold values from 0.5 to 1.5
- expert_ids: int32 [32768, 2], P(('seq', 'expert')), may hold values from 0 to 31, as said below
- gate_weights: float32 [32768, 2], P(('seq', 'expert')), may hold values from 0.1 to 1
- expert_in: bfloat16 [32, 1536, 4096], P('expert', None, 'seq'), may hold values from -0.15625 to 0.15625
- expert_out: bfloat16 [32, 4096, 1536], P('expert', 'seq'), may hold values from -0.09375 to 0.09375
- out_grad: bfloat16 [32768, 1536], P(('seq', 'expert')), may hold values from -6 to 6
Outputs:
- output: bfloat16 [32768, 1536], P(('seq', 'expert'))
- grad_latents: bfloat16 [32768, 1536], P(('seq', 'expert'))
- grad_control: bfloat16 [32768, 1536], P(('seq', 'expert'))
- grad_scale: float32 [1536], replicated
Inputs may be any that keep to these rules, and one draw needn't show every extreme that they name: `expert_ids`: the 2 experts of a token differ. On the rows of one device, 4 experts are named 24 times each, 8 are not named, and every other expert is named 2 * 128 // 32 times. In each aligned block of 4096 rows every expert is named exactly 2 * 128 times.
All inputs are finite; a program needn't handle non-finite values.
Results may differ from a plain program's by a relative error of at most 0.004.
Values may be sent and summed in bfloat16 or wider, within the bound.
A program may use at most 128 MiB of HBM per device.

v0:
```python
import jax
import jax.numpy as jnp
from jax import lax
from jax.sharding import PartitionSpec as P

coeff = 0.7978845608
cubic = 0.044715


def gelu_tanh(values):
    inner = jnp.tanh(coeff * (values + cubic * values * values * values))
    return 0.5 * values * (1.0 + inner)


def gelu_slope(values):
    inner = jnp.tanh(coeff * (values + cubic * values * values * values))
    return 0.5 * (1.0 + inner) + 0.5 * values * (1.0 - inner * inner) * coeff * (
        1.0 + 3.0 * cubic * values * values
    )


def body(
    latents,
    control,
    control_scale,
    norm_gain,
    expert_ids,
    gate_weights,
    expert_in,
    expert_out,
    out_grad,
):
    tokens, features = latents.shape
    routes_per = expert_ids.shape[1]
    experts = lax.axis_size("expert")
    capacity = 3 * routes_per * tokens // experts
    slot_count = experts * capacity
    live_rows = routes_per * tokens
    hidden_sum = latents.astype(jnp.float32) + control_scale * control.astype(jnp.float32)
    inverse = 1.0 / jnp.sqrt(jnp.mean(hidden_sum * hidden_sum, axis=-1, keepdims=True) + 1e-06)
    normed = hidden_sum * inverse
    routed = (normed * norm_gain).astype(jnp.bfloat16)
    flat_ids = expert_ids.reshape(-1)
    onehot = (flat_ids[:, None] == jnp.arange(experts, dtype=jnp.int32)[None, :]).astype(jnp.int32)
    slot_rank = jnp.sum((jnp.cumsum(onehot, axis=0) - 1) * onehot, axis=1)
    target = flat_ids * capacity + slot_rank
    owners = jnp.arange(live_rows, dtype=jnp.int32) // routes_per
    source = jnp.zeros((slot_count,), jnp.int32).at[target].set(owners)
    filled = (
        jnp.zeros((slot_count,), jnp.bfloat16).at[target].set(jnp.ones((live_rows,), jnp.bfloat16))
    )
    slot_marks = filled.reshape(experts, capacity)
    weight_in = lax.all_gather(expert_in, "seq", axis=2, tiled=True)[0]
    weight_out = lax.all_gather(expert_out, "seq", axis=1, tiled=True)[0]

    def pack_rows(values):
        picked = jnp.where(filled[:, None] > 0, values[source], jnp.zeros((), values.dtype))
        return picked.reshape(experts, capacity, features)

    def unpack_rows(values, chosen):
        spread = jnp.zeros((slot_count, features), values.dtype).at[chosen].set(values)
        return spread.reshape(experts, capacity, features)

    arrived_in, arrived_marks = (
        lax.all_to_all(pack_rows(routed), "expert", split_axis=0, concat_axis=0, tiled=True),
        lax.all_to_all(slot_marks, "expert", split_axis=0, concat_axis=0, tiled=True),
    )
    marked = arrived_marks.reshape(-1) > 0
    places = jnp.cumsum(marked.astype(jnp.int32)) - 1
    places = jnp.where(marked, places, live_rows)
    chosen = (
        jnp.zeros((live_rows,), jnp.int32)
        .at[places]
        .set(jnp.arange(slot_count, dtype=jnp.int32), mode="drop")
    )
    in_rows = arrived_in.reshape(slot_count, features)[chosen]
    pre_act = jnp.dot(in_rows, weight_in, preferred_element_type=jnp.float32)
    activated = gelu_tanh(pre_act).astype(jnp.bfloat16)
    result = jnp.dot(activated, weight_out, preferred_element_type=jnp.float32).astype(jnp.bfloat16)
    pre_act, result = (pre_act, result)
    returned_out = lax.all_to_all(
        unpack_rows(result, chosen), "expert", split_axis=0, concat_axis=0, tiled=True
    )
    arrived_grad = lax.all_to_all(
        pack_rows(out_grad), "expert", split_axis=0, concat_axis=0, tiled=True
    )
    grad_rows = arrived_grad.reshape(slot_count, features)[chosen]
    slope_back = jnp.dot(grad_rows, weight_out.T, preferred_element_type=jnp.float32) * gelu_slope(
        pre_act
    )
    slope_back = slope_back.astype(jnp.bfloat16)
    input_grad = jnp.dot(slope_back, weight_in.T, preferred_element_type=jnp.float32).astype(
        jnp.bfloat16
    )
    returned_grad = lax.all_to_all(
        unpack_rows(input_grad, chosen), "expert", split_axis=0, concat_axis=0, tiled=True
    )
    route_out = returned_out.reshape(slot_count, features)[target].reshape(
        tokens, routes_per, features
    )
    route_grad = returned_grad.reshape(slot_count, features)[target].reshape(
        tokens, routes_per, features
    )
    output = hidden_sum + jnp.sum(gate_weights[:, :, None] * route_out.astype(jnp.float32), axis=1)
    routed_grad = jnp.sum(gate_weights[:, :, None] * route_grad.astype(jnp.float32), axis=1)
    normed_grad = routed_grad * norm_gain
    sum_grad = inverse * (
        normed_grad - normed * jnp.mean(normed_grad * normed, axis=-1, keepdims=True)
    )
    sum_grad = sum_grad + out_grad.astype(jnp.float32)
    grad_latents = sum_grad.astype(jnp.bfloat16)
    grad_control = (sum_grad * control_scale).astype(jnp.bfloat16)
    local_scale = jnp.sum(sum_grad * control.astype(jnp.float32), axis=0)
    grad_scale = lax.psum(local_scale, ("seq", "expert"))
    return (output.astype(jnp.bfloat16), grad_latents, grad_control, grad_scale)


def solution(mesh):
    return jax.shard_map(
        body,
        mesh=mesh,
        in_specs=(
            P(("seq", "expert"), None),
            P(("seq", "expert"), None),
            P(),
            P(),
            P(("seq", "expert"), None),
            P(("seq", "expert"), None),
            P("expert", None, "seq"),
            P("expert", "seq", None),
            P(("seq", "expert"), None),
        ),
        out_specs=(
            P(("seq", "expert"), None),
            P(("seq", "expert"), None),
            P(("seq", "expert"), None),
            P(),
        ),
        check_vma=False,
    )
```

profile of v0, /device:TPU:1, one launch (start us, length us, event | category | flops | bytes accessed | tf_op | source)
XLA Modules:
  0.0 412.4 jit_solution(13784462016096934743)
XLA Ops:
  7.3 0.7 all-gather.3.cloned.1.call-update
  8.0 0.7 all-gather.5.cloned.1.call-update
  8.7 0.8 copy.21
  9.5 0.1 eq.29
  9.6 0.1 eq.25
  9.8 0.6 reduce-window.15
  10.4 0.2 slice_reduce_fusion
  10.6 0.7 broadcast_multiply_fusion
  11.3 0.1 copy.20
  11.4 0.1 mul.147
  11.7 2.2 scatter_custom_fusion
  13.8 0.7 all_to_all.24
  14.5 11.9 %all-to-all-start = ((bf16[32,1,24]{2,1,0:T(2,128)(2,1)}), bf16[32,1,24]{2,1,0:T(2,128)(2,1)S(1)}, u32[]{:S(2)}, u32[]{:S(2)}) async-start(bf16[32,1,24]{2,1,0:T(2,128)(2,1)} %all_to_all.24), calls=%async_computation | async-start | bytes 32768 | tf_op jit(solution)/shard_map/all_to_all | solution.py:66
  26.4 1.4 scatter_custom_fusion.2
  27.9 1.4 multiply_reduce_fusion.3
  29.3 0.2 multiply_convert_fusion.3
  29.5 3.8 gather_fusion
  33.4 3.9 gather_fusion.3
  37.3 4.3 %broadcast_select_fusion.1 = (bf16[32,24,1536]{2,1,0:T(8,128)(2,1)S(1)}, bf16[32,24,1536]{2,1,0:T(8,128)(2,1)}) fusion(bf16[32,24,1536]{2,1,0:T(8,128)(2,1)} %bitcast.62, pred[32,24]{1,0:T(8,128)(4,1)S(1)} %broadcast_in_dim.29, bf16[32,24,1536]{2,1,0:T(8,128)(2,1)} %bitcast.63), kind=kLoop, calls=%fused_computation.38 | loop fusion | flops 2359296 | bytes 9437952 | tf_op jit(solution)/shard_map/jit(_where)/select_n | solution.py:57
  41.6 65.0 %all_to_all.30 = bf16[32,24,1536]{2,1,0:T(8,128)(2,1)} all-to-all(bf16[32,24,1536]{2,1,0:T(8,128)(2,1)S(1)} %get-tuple-element.11), channel_id=1, replica_groups=mesh['seq'=8,'expert'=32] {'expert'}, dimensions={0} | all-to-all | bytes 4718592 | tf_op jit(solution)/shard_map/all_to_all | solution.py:65
  106.6 4.8 %all-to-all-start.3 = ((bf16[32,24,1536]{2,1,0:T(8,128)(2,1)}), bf16[32,24,1536]{2,1,0:T(8,128)(2,1)S(1)}, u32[]{:S(2)}, u32[]{:S(2)}) async-start(bf16[32,24,1536]{2,1,0:T(8,128)(2,1)} %get-tuple-element.12), calls=%async_computation.3 | async-start | bytes 4718592 | tf_op jit(solution)/shard_map/all_to_all | solution.py:84
  111.6 0.3 reduce-window.19
  112.1 0.1 slice_reduce_fusion.1
  112.4 3.5 scatter_custom_fusion.1
  115.9 0.6 pad_clamp_fusion.1
  116.5 4.2 %gather_fusion.1 = bf16[256,1536]{1,0:T(8,128)(2,1)S(1)} fusion(bf16[768,1536]{1,0:T(8,128)(2,1)} %bitcast.58, s32[1024]{0:T(1024)} %pad_clamp_fusion.1), kind=kCustom, calls=%fused_computation.1 | custom fusion | bytes 1573888 | tf_op jit(solution)/shard_map/gather | solution.py:76
  120.7 43.6 %all-to-all-done.3 = bf16[32,24,1536]{2,1,0:T(8,128)(2,1)S(1)} async-done(((bf16[32,24,1536]{2,1,0:T(8,128)(2,1)}), bf16[32,24,1536]{2,1,0:T(8,128)(2,1)S(1)}, u32[]{:S(2)}, u32[]{:S(2)}) %all-to-all-start.3) | async-done | bytes 2359328 | tf_op jit(solution)/shard_map/all_to_all | solution.py:84
  164.3 2.3 gather_fusion.4
  166.6 9.6 %fusion.6 = f32[256,4096]{1,0:T(8,128)} fusion(bf16[256,1536]{1,0:T(8,128)(2,1)S(1)} %gather_fusion.1, bf16[1,1536,4096]{2,1,0:T(8,128)(2,1)} %all-gather.3.cloned.1.call-done), kind=kOutput, calls=%fused_computation.17 | convolution fusion | flops 3221225472 | bytes 17563648 | tf_op jit(solution)/shard_map/dot_general | solution.py:77
  176.2 13.5 %fusion.31 = bf16[256,1536]{1,0:T(8,128)(2,1)S(1)} fusion(bf16[1,1536,4096]{2,1,0:T(8,128)(2,1)} %all-gather.3.cloned.1.call-done, bf16[256,1536]{1,0:T(8,128)(2,1)S(1)} %copy-done.5, bf16[1,4096,1536]{2,1,0:T(8,128)(2,1)} %all-gather.5.cloned.1.call-done, f32[256,4096]{1,0:T(8,128)} %fusion.6), kind=kOutput, calls=%fused_computation.36 | convolution fusion | flops 6462767104 | bytes 30932992 | tf_op jit(solution)/shard_map/dot_general | solution.py:92
  189.7 3.7 scatter_custom_fusion.4
  193.4 7.5 %all-to-all-start.4 = ((bf16[32,24,1536]{2,1,0:T(8,128)(2,1)}), bf16[32,24,1536]{2,1,0:T(8,128)(2,1)S(1)}, u32[]{:S(2)}, u32[]{:S(2)}) async-start(bf16[32,24,1536]{2,1,0:T(8,128)(2,1)} %bitcast.61), calls=%async_computation.4 | async-start | bytes 4718592 | tf_op jit(solution)/shard_map/all_to_all | solution.py:95
  200.9 10.4 %fusion.28 = bf16[256,1536]{1,0:T(8,128)(2,1)} fusion(bf16[1,4096,1536]{2,1,0:T(8,128)(2,1)} %all-gather.5.cloned.1.call-done, f32[256,4096]{1,0:T(8,128)} %fusion.6), kind=kOutput, calls=%fused_computation.35 | convolution fusion | flops 3231055872 | bytes 17563648 | tf_op jit(solution)/shard_map/dot_general | solution.py:79
  211.3 4.2 %scatter_custom_fusion.3 = bf16[768,1536]{1,0:T(8,128)(2,1)} fusion(s32[256]{0:T(256)} %copy-done.12, bf16[256,1536]{1,0:T(8,128)(2,1)} %fusion.28, bf16[]{:T(256)} %constant.19.clone.1), kind=kCustom, calls=%fused_computation.52 | custom fusion | bytes 2359808 | tf_op jit(solution)/shard_map/scatter | solution.py:61
  215.5 36.8 %all-to-all-done.4 = bf16[32,24,1536]{2,1,0:T(8,128)(2,1)S(1)} async-done(((bf16[32,24,1536]{2,1,0:T(8,128)(2,1)}), bf16[32,24,1536]{2,1,0:T(8,128)(2,1)S(1)}, u32[]{:S(2)}, u32[]{:S(2)}) %all-to-all-start.4) | async-done | bytes 2359328 | tf_op jit(solution)/shard_map/all_to_all | solution.py:95
  252.3 7.8 %all-to-all-start.2 = ((bf16[32,24,1536]{2,1,0:T(8,128)(2,1)}), bf16[32,24,1536]{2,1,0:T(8,128)(2,1)}, u32[]{:S(2)}, u32[]{:S(2)}) async-start(bf16[32,24,1536]{2,1,0:T(8,128)(2,1)} %bitcast.60), calls=%async_computation.2 | async-start | bytes 4718592 | tf_op jit(solution)/shard_map/all_to_all | solution.py:81
  260.1 0.7 copy.19
  260.8 0.6 pad_clamp_fusion
  261.4 1.4 gather_fusion.5
  262.8 1.0 reshape.192
  263.8 47.7 %all-to-all-done.2 = bf16[32,24,1536]{2,1,0:T(8,128)(2,1)} async-done(((bf16[32,24,1536]{2,1,0:T(8,128)(2,1)}), bf16[32,24,1536]{2,1,0:T(8,128)(2,1)}, u32[]{:S(2)}, u32[]{:S(2)}) %all-to-all-start.2) | async-done | bytes 2359328 | tf_op jit(solution)/shard_map/all_to_all | solution.py:81
  311.5 5.0 %gather_fusion.2 = bf16[256,1536]{1,0:T(8,128)(2,1)} fusion(bf16[768,1536]{1,0:T(8,128)(2,1)} %bitcast.8, s32[1024]{0:T(1024)} %pad_clamp_fusion), kind=kCustom, calls=%fused_computation.2 | custom fusion | bytes 1573888 | tf_op jit(solution)/shard_map/gather | solution.py:98
  316.5 2.2 reshape.191
  318.7 5.2 %multiply_reduce_fusion = (f32[128,1536]{1,0:T(8,128)S(1)}, f32[128,1536]{1,0:T(8,128)S(1)}) fusion(f32[128,2,1536]{2,1,0:T(2,128)S(1)} %reshape.192, f32[128,2]{1,0:T(8,128)} %copy.19, f32[128,2,1536]{2,1,0:T(2,128)S(1)} %reshape.191), kind=kLoop, calls=%fused_computation.48 | loop fusion | flops 1179648 | bytes 4719616 | tf_op jit(solution)/shard_map/reduce_sum | solution.py:105
  324.0 0.3 multiply_reduce_fusion.2
  324.3 1.2 fusion.50
  325.6 0.9 multiply_convert_fusion.2
  326.5 78.7 %psum.7 = f32[1536]{0:T(1024)} all-reduce(f32[1536]{0:T(1024)S(1)} %get-tuple-element.6), channel_id=1, replica_groups=mesh['seq'=8,'expert'=32] {'seq','expert'}, use_global_device_ids=true, to_apply=%region_15.16 | all-reduce | flops 1536 | bytes 12288 | tf_op jit(solution)/shard_map/psum | solution.py:114
  (56 shorter events, 0.9 us)
Async XLA Ops:
  7.2 22.1 %copy-start.1 = (bf16[128,1536]{1,0:T(8,128)(2,1)S(1)}, bf16[128,1536]{1,0:T(8,128)(2,1)}, u32[]{:S(2)}) copy-start(bf16[128,1536]{1,0:T(8,128)(2,1)} %param.10) | copy-start | bytes 1179652
  7.2 22.1 %copy-start.6 = (f32[1536]{0:T(1024)S(1)}, f32[1536]{0:T(1024)}, u32[]{:S(2)}) copy-start(f32[1536]{0:T(1024)} %param.11) | copy-start | bytes 18436
  7.2 22.1 %copy-start.3 = (bf16[128,1536]{1,0:T(8,128)(2,1)S(1)}, bf16[128,1536]{1,0:T(8,128)(2,1)}, u32[]{:S(2)}) copy-start(bf16[128,1536]{1,0:T(8,128)(2,1)} %param.9) | copy-start | bytes 1179652
  7.2 22.1 %copy-start.7 = (f32[1536]{0:T(1024)S(1)}, f32[1536]{0:T(1024)}, u32[]{:S(2)}) copy-start(f32[1536]{0:T(1024)} %param.12) | copy-start | bytes 18436
  7.2 159.4 %all-gather.3.cloned.1.call-start = ((), (), s32[]{:S(2)}) async-start(), calls=%async_computation.5 | async-start | bytes 14155776 | tf_op jit(solution)/shard_map/all_gather | solution.py:53
  7.9 168.3 %all-gather.5.cloned.1.call-start = ((), (), s32[]{:S(2)}) async-start(), calls=%async_computation.6 | async-start | bytes 14155776 | tf_op jit(solution)/shard_map/all_gather | solution.py:54
  11.7 17.6 %copy-start.10 = (s32[256,1]{0,1:T(1,128)}, s32[256,1]{0,1:T(1,128)S(1)}, u32[]{:S(2)}) copy-start(s32[256,1]{0,1:T(1,128)S(1)} %compare_select_fusion.2) | copy-start | bytes 3076
  14.5 27.0 %all-to-all-start = ((bf16[32,1,24]{2,1,0:T(2,128)(2,1)}), bf16[32,1,24]{2,1,0:T(2,128)(2,1)S(1)}, u32[]{:S(2)}, u32[]{:S(2)}) async-start(bf16[32,1,24]{2,1,0:T(2,128)(2,1)} %all_to_all.24), calls=%async_computation | async-start | bytes 32768 | tf_op jit(solution)/shard_map/all_to_all | solution.py:66
  29.3 4.0 copy-start.8
  29.5 3.8 copy-start
  106.6 57.7 %all-to-all-start.3 = ((bf16[32,24,1536]{2,1,0:T(8,128)(2,1)}), bf16[32,24,1536]{2,1,0:T(8,128)(2,1)S(1)}, u32[]{:S(2)}, u32[]{:S(2)}) async-start(bf16[32,24,1536]{2,1,0:T(8,128)(2,1)} %get-tuple-element.12), calls=%async_computation.3 | async-start | bytes 4718592 | tf_op jit(solution)/shard_map/all_to_all | solution.py:84
  115.9 0.6 copy-start.12
  166.6 9.6 %copy-start.5 = (bf16[256,1536]{1,0:T(8,128)(2,1)S(1)}, bf16[256,1536]{1,0:T(8,128)(2,1)}, u32[]{:S(2)}) copy-start(bf16[256,1536]{1,0:T(8,128)(2,1)} %gather_fusion.4) | copy-start | bytes 2359300
  193.4 58.9 %all-to-all-start.4 = ((bf16[32,24,1536]{2,1,0:T(8,128)(2,1)}), bf16[32,24,1536]{2,1,0:T(8,128)(2,1)S(1)}, u32[]{:S(2)}, u32[]{:S(2)}) async-start(bf16[32,24,1536]{2,1,0:T(8,128)(2,1)} %bitcast.61), calls=%async_computation.4 | async-start | bytes 4718592 | tf_op jit(solution)/shard_map/all_to_all | solution.py:95
  211.3 48.8 %copy-start.13 = (f32[128,2]{0,1:T(2,128)S(1)}, f32[128,2]{0,1:T(2,128)}, u32[]{:S(2)}) copy-start(f32[128,2]{0,1:T(2,128)} %param.14) | copy-start | bytes 3076
  211.3 49.5 %copy-start.11 = (s32[256,1]{0,1:T(1,128)S(1)}, s32[256,1]{0,1:T(1,128)}, u32[]{:S(2)}) copy-start(s32[256,1]{0,1:T(1,128)} %copy-done.10) | copy-start | bytes 3076
  252.3 59.2 %all-to-all-start.2 = ((bf16[32,24,1536]{2,1,0:T(8,128)(2,1)}), bf16[32,24,1536]{2,1,0:T(8,128)(2,1)}, u32[]{:S(2)}, u32[]{:S(2)}) async-start(bf16[32,24,1536]{2,1,0:T(8,128)(2,1)} %bitcast.60), calls=%async_computation.2 | async-start | bytes 4718592 | tf_op jit(solution)/shard_map/all_to_all | solution.py:81
  318.7 5.3 %copy-start.2 = (bf16[128,1536]{1,0:T(8,128)(2,1)S(1)}, bf16[128,1536]{1,0:T(8,128)(2,1)}, u32[]{:S(2)}) copy-start(bf16[128,1536]{1,0:T(8,128)(2,1)} %param.10) | copy-start | bytes 1179652
  318.7 5.3 %copy-start.4 = (bf16[128,1536]{1,0:T(8,128)(2,1)S(1)}, bf16[128,1536]{1,0:T(8,128)(2,1)}, u32[]{:S(2)}) copy-start(bf16[128,1536]{1,0:T(8,128)(2,1)} %param.9) | copy-start | bytes 1179652
  318.7 5.3 %copy-start.9 = (f32[128]{0:T(128)S(1)}, f32[128]{0:T(128)}, u32[]{:S(2)}) copy-start(f32[128]{0:T(128)} %copy-done.8) | copy-start | bytes 1540
Sparse Core Ops, SparseCore 0:
  9.9 74.0 all-gather.2
  85.9 70.3 all-gather.4
where the time goes:
time: 420 us; the launch traced here: 412 us
  blocking collectives  144 us (34%)
  waiting for transfers between devices  130 us (31%)
  local copies, waits for them, and re-layouts  42.2 us (10%)
  matrix products  33.5 us (8%)
  starting transfers between devices  32 us (8%)
  other arithmetic  16.8 us (4%)
  between operations  14.8 us (4%)
    psum x1, blocking collectives, body(): grad_scale = lax.psum(local_scale, ('seq', 'expert'))  78.7 us
    all_to_all x1, blocking collectives, body(): lax.all_to_all(pack_rows(routed), 'expert', split_axis=0, concat_axis=0,...  65 us
    all_to_all x1, waiting for transfers between devices, body(): lax.all_to_all(unpack_rows(result, chosen), 'expert', split_axis=0, conca...  47.7 us
    all_to_all x1, waiting for transfers between devices, body(): lax.all_to_all(pack_rows(out_grad), 'expert', split_axis=0, concat_axis=0...  43.6 us
    all_to_all x1, waiting for transfers between devices, body(): lax.all_to_all(unpack_rows(input_grad, chosen), 'expert', split_axis=0, c...  36.8 us
    dot_general x1, matrix products, body(): jnp.dot(slope_back, weight_in.T, preferred_element_type=jnp.float32)  13.5 us
    all_to_all x1, starting transfers between devices, body(): lax.all_to_all(slot_marks, 'expert', split_axis=0, concat_axis=0, tiled=T...  11.9 us
    dot_general x1, matrix products, body(): jnp.dot(activated, weight_out, preferred_element_type=jnp.float32)  10.4 us
  transfers between devices with their start and end apart: 6, of which 3 were waited for; matrix products, arithmetic and copies ran while one was open for 14% of the time, Pallas kernels for 0%

commit v1 on v0

v1 whole, which is shorter than its diff:
```python
import jax
import jax.numpy as jnp
from jax import lax
from jax.experimental import pallas as pl
from jax.experimental.pallas import tpu as pltpu
from jax.sharding import PartitionSpec as P

coeff = 0.7978845608
cubic = 0.044715

MESH = pl.DeviceIdType.MESH
BF = jnp.bfloat16
F32 = jnp.float32

T = 128
CAP = 24
PAIR = 2 * CAP
ROWS = 256
D = 1536
SH = 512
HID = 2 * SH
RES, GRAD = 0, 1
NT = 256
Z_SLOT = {1: 2, 2: 4, 3: 6, 4: 1, 5: 7, 6: 5, 7: 3}


def nn(a, b):
    return lax.dot_general(a, b, (((1,), (0,)), ((), ())), preferred_element_type=F32)


def nt(a, b):
    return lax.dot_general(a, b, (((1,), (1,)), ((), ())), preferred_element_type=F32)


def tn(a, b):
    return lax.dot_general(a, b, (((0,), (0,)), ((), ())), preferred_element_type=F32)


def iota(shape, dim):
    return lax.broadcasted_iota(jnp.int32, shape, dim)


class Wires:
    def __init__(self, send, recv):
        self.send, self.recv = send, recv
        self.copies = {}
        self.sent = set()

    def start(self, key, src, dst, device):
        place = len(self.copies)
        copy = pltpu.make_async_remote_copy(
            src_ref=src,
            dst_ref=dst,
            send_sem=self.send.at[place],
            recv_sem=self.recv.at[place],
            device_id=device,
            device_id_type=MESH,
        )
        copy.start()
        self.copies[key] = copy

    def arrived(self, key):
        self.copies[key].wait_recv()

    def left(self, key):
        if key not in self.sent:
            self.sent.add(key)
            self.copies[key].wait_send()

    def finish(self):
        for key in self.copies:
            self.left(key)


N_COPIES = 14 + 7 + 3 + 2 + 14 + 24 + 6 + 6 + 24 + 28 + 14


def kernel(
    meta_ref, lat_ref, ctl_ref, og_ref, cs_ref, ng_ref, wi_ref, wo_ref,
    out_ref, gl_ref, gc_ref, gs_ref,
    zb, xst, xsl, rows, wi, wo, act, slope, fr, fin, pb, pown, own, codes, pick, meta, hid, gb,
    send, recv, lsem, free,
):
    me_s, me_e = lax.axis_index("seq"), lax.axis_index("expert")
    y, c = lax.div(me_s, 2), lax.rem(me_s, 2)
    z, x = lax.div(me_e, 4), lax.rem(me_e, 4)

    def z_at(delta):
        return (me_s, lax.rem(z + delta + 8, 8) * 4 + x)

    def x_at(delta):
        return (me_s, z * 4 + lax.rem(x + delta + 4, 4))

    def y_at(delta):
        return (lax.rem(y + delta, 4) * 2 + c, me_e)

    odd = lax.rem(y, 2)
    sibling = (y * 2 + 1 - c, me_e)
    w_mate = ((y + 1 - 2 * odd) * 2 + c, me_e)
    t_mate = (lax.rem(y + 3 + 2 * odd, 4) * 2 + c, me_e)
    peers = [z_at(k) for k in range(1, 8)] + [x_at(k) for k in range(1, 4)]
    peers += [y_at(k) for k in range(1, 4)] + [sibling]

    barrier = pltpu.get_barrier_semaphore()
    for peer in peers:
        pl.semaphore_signal(barrier, inc=1, device_id=peer, device_id_type=MESH)

    own_in = pltpu.make_async_copy(wi_ref.at[0], wi.at[:, pl.ds(0, SH)], lsem.at[0])
    own_out = pltpu.make_async_copy(wo_ref.at[0], wo.at[pl.ds(0, SH), :], lsem.at[1])
    own_in.start()
    own_out.start()

    hidden = lat_ref[...].astype(F32) + cs_ref[...] * ctl_ref[...].astype(F32)
    hid[...] = hidden
    inverse = 1.0 / jnp.sqrt(jnp.mean(hidden * hidden, axis=-1, keepdims=True) + 1e-06)
    zb[RES, 0:T] = (hidden * inverse * ng_ref[...]).astype(BF)
    zb[GRAD, 0:T] = og_ref[...]

    id0, id1 = meta_ref[0:1], meta_ref[1:2]
    labels = iota((32, T), 0).astype(F32)
    hot0 = jnp.where(id0 == labels, 1.0, 0.0)
    hot1 = jnp.where(id1 == labels, 1.0, 0.0)
    before = jnp.where(iota((T, T), 0) < iota((T, T), 1), 1.0, 0.0).astype(BF)
    rank0 = jnp.sum(hot0 * nn(hot0.astype(BF), before), axis=0, keepdims=True)
    ahead = jnp.sum(hot0, axis=1, keepdims=True)
    rank1 = jnp.sum(hot1 * (nn(hot1.astype(BF), before) + ahead), axis=0, keepdims=True)
    line = iota((8, T), 0)
    meta[0, 0:8] = jnp.where(
        line == 0, id0 * CAP + rank0, jnp.where(line == 1, id1 * CAP + rank1, meta_ref[...])
    )

    pl.semaphore_wait(barrier, len(peers))
    wires = Wires(send, recv)

    def z_own(a):
        for h in range(2):
            for side in range(2):
                wires.start(
                    ("z", a, side, h),
                    zb.at[a, pl.ds(64 * h, 64)],
                    zb.at[a, pl.ds(256 + T * side + 64 * h, 64)],
                    z_at(1 - 2 * side),
                )

    def z_forward(a, d):
        for h in range(2):
            for side in range(2):
                wires.arrived(("z", a, side, 2 * (d - 1) + h))
                src = zb.at[a, pl.ds(256 * d + T * side + 64 * h, 64)]
                if d < 3:
                    dst = zb.at[a, pl.ds(256 * (d + 1) + T * side + 64 * h, 64)]
                    wires.start(("z", a, side, 2 * d + h), src, dst, z_at(1 - 2 * side))
                elif side == h:
                    dst = zb.at[a, pl.ds(T + 64 * h, 64)]
                    wires.start(("z", a, side, 6), src, dst, z_at(1 - 2 * side))

    def targets(g, k):
        return jnp.concatenate(
            [meta[0, pl.ds(16 * g + k, 1)], meta[0, pl.ds(16 * g + 8 + k, 1)]], axis=1
        )

    def select(a, g):
        one = jnp.where(codes[...] == targets(g, 0), 1.0, 0.0)
        one = jnp.where(codes[...] == targets(g, 1), 1.0, one).astype(BF)
        for n in range(0, D, 512):
            got = nn(one, zb[a, pl.ds(256 * g, 256), pl.ds(n, 512)]).astype(BF)
            xsl[a, pl.ds(PAIR * g, PAIR), pl.ds(n, 512)] = got[0:PAIR]
            xst[a, g, pl.ds(PAIR, 3 * PAIR), pl.ds(n, 512)] = got[PAIR:]
        for j in range(1, 4):
            wires.start(
                ("x", a, j, g),
                xst.at[a, g, pl.ds(PAIR * j, PAIR)],
                xsl.at[a, pl.ds((4 * j + g) * PAIR, PAIR)],
                x_at(j),
            )

    def compact(a):
        for j in range(1, 4):
            for g in range(4):
                wires.left(("x", a, j, g))
            pl.semaphore_signal(free.at[a], inc=1, device_id=x_at(j), device_id_type=MESH)
        for j in range(1, 4):
            for g in range(4):
                wires.arrived(("x", a, j, g))
        for n in range(0, D, 512):
            rows[a, 0:ROWS, pl.ds(n, 512)] = nn(pick[...], xsl[a, :, pl.ds(n, 512)]).astype(BF)
        wires.start(
            ("e", a, 2), rows.at[a, pl.ds(0, ROWS)], rows.at[a, pl.ds(2 * ROWS, ROWS)], t_mate
        )
        wires.start(
            ("e", a, 1), rows.at[a, pl.ds(0, ROWS)], rows.at[a, pl.ds(ROWS, ROWS)], sibling
        )

    def pass_rows(a):
        wires.arrived(("e", a, 2))
        wires.start(
            ("e", a, 3),
            rows.at[a, pl.ds(2 * ROWS, ROWS)],
            rows.at[a, pl.ds(3 * ROWS, ROWS)],
            sibling,
        )

    def half(p):
        return pl.ds(2 * ROWS * p, 2 * ROWS)

    def forward(p):
        @pl.loop(0, HID // NT)
        def _(i):
            cols = pl.ds(pl.multiple_of(i * NT, NT), NT)
            v = nn(rows[RES, half(p)], wi[:, cols])
            inner = jnp.tanh(coeff * (v + cubic * v * v * v))
            act[half(p), cols] = (0.5 * v * (1.0 + inner)).astype(BF)
            slope[half(p), cols] = 0.5 * (1.0 + inner) + 0.5 * v * (1.0 - inner * inner) * coeff * (
                1.0 + 3.0 * cubic * v * v
            )

    def result(p):
        @pl.loop(0, D // NT)
        def _(i):
            cols = pl.ds(pl.multiple_of(i * NT, NT), NT)
            zb[RES, half(p), cols] = nn(act[half(p), :], wo[:, cols]).astype(BF)

    def backward(p):
        @pl.loop(0, HID // NT)
        def _(i):
            cols = pl.ds(pl.multiple_of(i * NT, NT), NT)
            act[half(p), cols] = (nt(rows[GRAD, half(p)], wo[cols, :]) * slope[half(p), cols]).astype(BF)

    def input_grad(p):
        @pl.loop(0, D // NT)
        def _(i):
            cols = pl.ds(pl.multiple_of(i * NT, NT), NT)
            zb[GRAD, half(p), cols] = nt(act[half(p), :], wi[cols, :]).astype(BF)

    def part(a, o):
        return zb.at[a, pl.ds(ROWS * o, ROWS)]

    def part_to_sibling(a, o):
        wires.start(("f", a, o), part(a, o), fr.at[a, 2 if o == 3 else 0], sibling)

    def part_to_mate(a):
        wires.arrived(("f", a, 3))
        zb[a, pl.ds(2 * ROWS, ROWS)] = (
            zb[a, pl.ds(2 * ROWS, ROWS)].astype(F32) + fr[a, 2].astype(F32)
        ).astype(BF)
        wires.start(("f", a, 2), part(a, 2), fr.at[a, 1], t_mate)

    def give_back(a):
        wires.arrived(("f", a, 1))
        wires.arrived(("f", a, 2))
        fin[...] = (
            zb[a, 0:ROWS].astype(F32) + fr[a, 0].astype(F32) + fr[a, 1].astype(F32)
        ).astype(BF)
        for n in range(0, D, 512):
            got = tn(pick[...], fin[:, pl.ds(n, 512)]).astype(BF)
            for g in range(4):
                xst[a, g, 0:PAIR, pl.ds(n, 512)] = got[PAIR * g : PAIR * (g + 1)]
            xsl[a, pl.ds(4 * PAIR, 12 * PAIR), pl.ds(n, 512)] = got[4 * PAIR :]
        pl.semaphore_wait(free.at[a], 3)
        for g in (0, 3, 2, 1):
            for j in range(1, 4):
                wires.start(
                    ("r", a, j, g),
                    xsl.at[a, pl.ds((4 * j + g) * PAIR, PAIR)],
                    xst.at[a, g, pl.ds(PAIR * j, PAIR)],
                    x_at(-j),
                )

    def gathered(a, g):
        for j in range(1, 4):
            wires.arrived(("r", a, j, g))
        gate = jnp.where(codes[...] == targets(g, 0), targets(g, 2), 0.0)
        gate = jnp.where(codes[...] == targets(g, 1), targets(g, 3), gate)
        high = gate.astype(BF)
        low = (gate - high.astype(F32)).astype(BF)

        def columns(n):
            got = xst[a, g, :, pl.ds(n, 512)]
            return tn(high, got) + tn(low, got)

        return columns

    def z_back(a, g, side, h, m):
        src = zb_back(a, g, side, h)
        dst = pb.at[a, pl.ds(256 * (g - 1) + T * side + 64 * h, 64)]
        wires.start(("b", a, side, m), src, dst, z_at(2 * side - 1))

    def zb_back(a, g, side, h):
        if g == 4:
            return pown.at[a, pl.ds(64 * h, 64)]
        return pb.at[a, pl.ds(256 * g + T * side + 64 * h, 64)]

    def reduce_first(a):
        columns = gathered(a, 0)
        for n in range(0, D, 512):
            got = columns(n)
            own[a, :, pl.ds(n, 512)] = got[0:T]
            pown[a, :, pl.ds(n, 512)] = got[T:].astype(BF)
        z_back(a, 4, 0, 0, 0)
        z_back(a, 4, 1, 1, 0)

    def reduce_next(a, g):
        columns = gathered(a, g)
        base = 256 * g
        if g == 3:
            for side in range(2):
                wires.arrived(("b", a, side, 0))
        else:
            for side in range(2):
                for h in range(2):
                    wires.arrived(("b", a, side, 5 - 2 * g + h))
        for n in range(0, D, 512):
            got = columns(n)
            spans = ((0, 64, True), (64, 128, False), (192, 64, True)) if g == 3 else ((0, 256, True),)
            for at, size, add in spans:
                value = got[at : at + size]
                if add:
                    value = value + pb[a, pl.ds(base + at, size), pl.ds(n, 512)].astype(F32)
                pb[a, pl.ds(base + at, size), pl.ds(n, 512)] = value.astype(BF)
        for h in range(2):
            for side in range(2):
                z_back(a, g, side, h, 7 - 2 * g + h)

    def reduce_last(a):
        for side in range(2):
            for h in range(2):
                wires.arrived(("b", a, side, 5 + h))
        return own[a] + pb[a, 0:T].astype(F32) + pb[a, T:256].astype(F32)


    z_own(RES)
    for k in range(1, 8):
        wires.start(("mz", k), meta.at[0, pl.ds(0, 8)], meta.at[0, pl.ds(8 * Z_SLOT[k], 8)], z_at(k))
    wires.start(("w", 0), wi_ref.at[0], wi.at[:, pl.ds(SH, SH)], w_mate)
    wires.start(("w", 1), wo_ref.at[0], wo.at[pl.ds(SH, SH), :], w_mate)
    spot = iota((PAIR, 256), 0)
    spot = jnp.where(spot >= CAP, spot - CAP + 1024, spot)
    spot = spot - jnp.where(iota((PAIR, 256), 1) >= T, 1024, 0)
    spot = jnp.where((spot >= 0) & (spot < CAP), spot, -65536).astype(F32)
    for j in range(4):
        first = (z * 4 + lax.rem(x + j, 4)) * CAP
        codes[pl.ds(PAIR * j, PAIR)] = spot + first.astype(F32)
    for k in range(1, 8):
        wires.arrived(("mz", k))
    for j in range(1, 4):
        wires.start(("mx", j), meta.at[0], meta.at[j], x_at(j))

    for d in (1, 2, 3):
        z_forward(RES, d)
        if d == 3:
            z_own(GRAD)
        select(RES, d)
    for side in range(2):
        wires.arrived(("z", RES, side, 6))
    select(RES, 0)

    for j in range(1, 4):
        wires.arrived(("mx", j))
    marks = meta[...].reshape(256, T)
    low = (me_e * CAP).astype(F32)
    named = (marks >= low) & (marks < low + CAP) & ((iota((256, T), 0) & 7) < 2)
    named = jnp.where(named, 1.0, 0.0).astype(BF)
    counts = nt(jnp.ones((8, T), BF), named).astype(BF)
    begin = (iota((256, 4 * PAIR * 4), 0) >> 3) * CAP
    slot = iota((256, 4 * PAIR * 4), 1)
    inside = (slot >= begin) & (slot < begin + CAP)
    filled = nn(counts, jnp.where(inside, 1.0, 0.0).astype(BF))
    offset = nn(counts, jnp.where(slot >= begin + CAP, 1.0, 0.0).astype(BF))
    slot = iota((8, 4 * PAIR * 4), 1).astype(F32)
    rank = slot - CAP * jnp.floor((slot + 0.5) * (1.0 / CAP))
    place = jnp.where(rank < filled, offset + rank, -1.0)
    pick[...] = jnp.where(iota((ROWS, 4 * PAIR * 4), 0).astype(F32) == place[0:1], 1.0, 0.0).astype(BF)

    z_forward(GRAD, 1)
    compact(RES)
    select(GRAD, 1)
    z_forward(GRAD, 2)
    pass_rows(RES)
    select(GRAD, 2)
    own_in.wait()
    wires.arrived(("w", 0))
    wires.arrived(("e", RES, 1))
    forward(0)
    z_forward(GRAD, 3)
    select(GRAD, 3)
    wires.arrived(("e", RES, 3))
    forward(1)
    for side in range(2):
        wires.arrived(("z", GRAD, side, 6))
    select(GRAD, 0)
    own_out.wait()
    wires.arrived(("w", 1))
    for side in range(2):
        for m in range(7):
            wires.left(("z", RES, side, m))
    result(1)
    part_to_sibling(RES, 3)
    result(0)
    part_to_sibling(RES, 1)
    compact(GRAD)
    part_to_mate(RES)
    pass_rows(GRAD)
    wires.arrived(("e", GRAD, 1))
    backward(0)
    give_back(RES)
    wires.arrived(("e", GRAD, 3))
    backward(1)
    for side in range(2):
        for m in range(7):
            wires.left(("z", GRAD, side, m))
    input_grad(1)
    part_to_sibling(GRAD, 3)
    input_grad(0)
    part_to_sibling(GRAD, 1)
    reduce_first(RES)
    part_to_mate(GRAD)
    reduce_next(RES, 3)
    give_back(GRAD)
    reduce_next(RES, 2)
    reduce_first(GRAD)
    reduce_next(RES, 1)
    reduce_next(GRAD, 3)
    out_ref[...] = (hid[...] + reduce_last(RES)).astype(BF)
    reduce_next(GRAD, 2)
    reduce_next(GRAD, 1)

    hidden = hid[...]
    inverse = 1.0 / jnp.sqrt(jnp.mean(hidden * hidden, axis=-1, keepdims=True) + 1e-06)
    normed = hidden * inverse
    normed_grad = reduce_last(GRAD) * ng_ref[...]
    mean = jnp.mean(normed_grad * normed, axis=-1, keepdims=True)
    sum_grad = inverse * (normed_grad - normed * mean) + og_ref[...].astype(F32)
    gl_ref[...] = sum_grad.astype(BF)
    gc_ref[...] = (sum_grad * cs_ref[...]).astype(BF)

    total = jnp.sum(sum_grad * ctl_ref[...].astype(F32), axis=0, keepdims=True)
    stages = (
        (0, 8, z, [z_at(k) for k in range(1, 8)]),
        (8, 4, x, [x_at(k) for k in range(1, 4)]),
        (12, 4, y, [y_at(k) for k in range(1, 4)]),
        (16, 2, c, [sibling]),
    )
    for base, size, mine, others in stages:
        gb[base + mine] = total
        for k, other in enumerate(others):
            wires.start(("g", base, k), gb.at[base + mine], gb.at[base + mine], other)
        for k in range(len(others)):
            wires.arrived(("g", base, k))
        total = gb[base]
        for k in range(1, size):
            total = total + gb[base + k]
    gs_ref[...] = total
    wires.finish()


def body(
    latents, control, control_scale, norm_gain, expert_ids, gate_weights, expert_in, expert_out, out_grad
):
    marks = jnp.concatenate(
        [expert_ids.T.astype(F32), gate_weights.T, jnp.zeros((4, T), F32)], axis=0
    )
    vmem = pl.BlockSpec(memory_space=pltpu.VMEM)
    hbm = pl.BlockSpec(memory_space=pl.ANY)
    output, grad_latents, grad_control, grad_scale = pl.pallas_call(
        kernel,
        out_shape=(
            jax.ShapeDtypeStruct((T, D), BF),
            jax.ShapeDtypeStruct((T, D), BF),
            jax.ShapeDtypeStruct((T, D), BF),
            jax.ShapeDtypeStruct((1, D), F32),
        ),
        in_specs=[vmem] * 6 + [hbm] * 2,
        out_specs=(vmem,) * 4,
        scratch_shapes=[
            pltpu.VMEM((2, 4 * 256, D), BF),
            pltpu.VMEM((2, 4, 4 * PAIR, D), BF),
            pltpu.VMEM((2, 16 * PAIR, D), BF),
            pltpu.VMEM((2, 4 * ROWS, D), BF),
            pltpu.VMEM((D, HID), BF),
            pltpu.VMEM((HID, D), BF),
            pltpu.VMEM((4 * ROWS, HID), BF),
            pltpu.VMEM((4 * ROWS, HID), F32),
            pltpu.VMEM((2, 3, ROWS, D), BF),
            pltpu.VMEM((ROWS, D), BF),
            pltpu.VMEM((2, 4 * 256, D), BF),
            pltpu.VMEM((2, T, D), BF),
            pltpu.VMEM((2, T, D), F32),
            pltpu.VMEM((4 * PAIR, 256), F32),
            pltpu.VMEM((ROWS, 16 * PAIR), BF),
            pltpu.VMEM((4, 64, T), F32),
            pltpu.VMEM((T, D), F32),
            pltpu.VMEM((18, 1, D), F32),
            pltpu.SemaphoreType.DMA((N_COPIES,)),
            pltpu.SemaphoreType.DMA((N_COPIES,)),
            pltpu.SemaphoreType.DMA((2,)),
            pltpu.SemaphoreType.REGULAR((2,)),
        ],
        compiler_params=pltpu.CompilerParams(
            collective_id=0, has_side_effects=True, vmem_limit_bytes=63 * 1024 * 1024
        ),
    )(
        marks, latents, control, out_grad, control_scale[None, :], norm_gain[None, :],
        expert_in, expert_out,
    )
    return output, grad_latents, grad_control, grad_scale[0]


def solution(mesh):
    return jax.shard_map(
        body,
        mesh=mesh,
        in_specs=(
            P(("seq", "expert"), None),
            P(("seq", "expert"), None),
            P(),
            P(),
            P(("seq", "expert"), None),
            P(("seq", "expert"), None),
            P("expert", None, "seq"),
            P("expert", "seq", None),
            P(("seq", "expert"), None),
        ),
        out_specs=(
            P(("seq", "expert"), None),
            P(("seq", "expert"), None),
            P(("seq", "expert"), None),
            P(),
        ),
        check_vma=False,
    )
```

time: 420 us -> 233 us (0.55); the launches traced: 412 us -> 232 us
  Pallas kernels: 0 us -> 221 us
  blocking collectives: 144 us -> 0 us
  waiting for transfers between devices: 130 us -> 0 us
  local copies, waits for them, and re-layouts: 42.2 us -> 6.95 us
  matrix products: 33.5 us -> 0 us
  starting transfers between devices: 32 us -> 0 us
  between operations: 14.8 us -> 0.65 us
  other arithmetic: 16.8 us -> 3.38 us
    pallas_call x0 -> x1, Pallas kernels: none -> 221 us  [body(): pl.pallas_call(kernel, out_shape=(jax.ShapeDtypeStruct((T, D), BF), jax.S...]
    all_to_all x4 -> x0, waiting for transfers between devices: 128 us -> none  [the longest x1 47.7 us: body(): lax.all_to_all(unpack_rows(result, chosen), 'expert', split_axis=0, conca...]
    psum x1 -> x0, blocking collectives: 78.7 us -> none  [body(): grad_scale = lax.psum(local_scale, ('seq', 'expert'))]
    all_to_all x1 -> x0, blocking collectives: 65 us -> none  [body(): lax.all_to_all(pack_rows(routed), 'expert', split_axis=0, concat_axis=0,...]
    dot_general x3 -> x0, matrix products: 33.5 us -> none  [the longest x1 13.5 us: body(): jnp.dot(slope_back, weight_in.T, preferred_element_type=jnp.float32)]
    all_to_all x4 -> x0, starting transfers between devices: 31.9 us -> none  [the longest x1 11.9 us: body(): lax.all_to_all(slot_marks, 'expert', split_axis=0, concat_axis=0, tiled=T...]
    gather x6 -> x0, local copies, waits for them, and re-layouts: 20.5 us -> none  [the longest x2 7.68 us: pack_rows(): values[source]]
    scatter x5 -> x0, local copies, waits for them, and re-layouts: 15 us -> none  [the longest x2 7.92 us: unpack_rows(): jnp.zeros((slot_count, features), values.dtype).at[chosen].set(values)]
  transfers between devices with their start and end apart: 6 -> 0, of which waited for: 3 -> 0; matrix products, arithmetic and copies ran while one was open for 14% -> 0% of each run, Pallas kernels for 0% -> 0%
where the time goes in v1:
time: 233 us; the launch traced here: 232 us
  Pallas kernels  221 us (95%)
  local copies, waits for them, and re-layouts  6.95 us (3%)
  other arithmetic  3.38 us (1%)
    pallas_call x1, Pallas kernels, body(): pl.pallas_call(kernel, out_shape=(jax.ShapeDtypeStruct((T, D), BF), jax.S...  221 us

profile of v1, /device:TPU:1, one launch (start us, length us, event | category | flops | bytes accessed | tf_op | source)
XLA Modules:
  0.0 232.0 jit_solution(7366443471863718826)
XLA Ops:
  0.6 1.3 broadcast_in_dim.10.cs_ref
  1.9 1.3 broadcast_in_dim.11.ng_ref
  3.2 0.7 convert_bitcast_fusion
  3.9 0.1 pad.2.clone
  4.0 1.3 maximum_maximum_fusion.meta_ref
  5.3 221.1 %shard_map.120 = (bf16[128,1536]{1,0:T(8,128)(2,1)}, bf16[128,1536]{1,0:T(8,128)(2,1)}, bf16[128,1536]{1,0:T(8,128)(2,1)}, f32[1,1536]{1,0:T(1,128)}) custom-call(f32[8,128]{1,0:T(8,128)} %maximum_maximum_fusion.meta_ref, bf16[128,1536]{1,0:T(8,128)(2,1)} %lat_ref.1, bf16[128,1536]{1,0:T(8,128)(2,1)} %ctl_ref.1, bf16[128,1536]{1,0:T(8,128)(2,1)} %og_ref.1, ...), custom_call_target="tpu_custom_call" | custom-call | tf_op jit(solution)/shard_map/pallas_call | solution.py:464
  226.4 0.0 copy-start
  226.4 1.4 reduce
  227.8 1.8 copy.16
  229.5 1.8 copy.17
  231.3 0.0 copy-done
  231.3 0.7 copy.18
  (1 shorter events, 0.0 us)
Async XLA Ops:
  226.4 4.9 %copy-start = (bf16[128,1536]{1,0:T(8,128)(2,1)S(1)}, bf16[128,1536]{1,0:T(8,128)(2,1)}, u32[]{:S(2)}) copy-start(bf16[128,1536]{1,0:T(8,128)(2,1)} %get-tuple-element.18) | copy-start | bytes 1179652

commit v2 on v1

v2 whole, which is shorter than its diff:
```python
import jax
import jax.numpy as jnp
from jax import lax
from jax.experimental import pallas as pl
from jax.experimental.pallas import tpu as pltpu
from jax.sharding import PartitionSpec as P

coeff = 0.7978845608
cubic = 0.044715

MESH = pl.DeviceIdType.MESH
BF = jnp.bfloat16
F32 = jnp.float32

T = 128
CAP = 24
PAIR = 2 * CAP
ROWS = 256
D = 1536
SH = 512
HID = 2 * SH
RES, GRAD = 0, 1
NT = 256
Q = D // 2
N_SLOT = 32 * CAP
BLOCKS = {0: (0, 0, 0, HID), 1: (2 * ROWS, 2 * ROWS, 0, SH), 2: (4 * ROWS, 2 * ROWS, SH, HID)}
Z_SLOT = {1: 2, 2: 4, 3: 6, 4: 1, 5: 7, 6: 5, 7: 3}


def nn(a, b):
    return lax.dot_general(a, b, (((1,), (0,)), ((), ())), preferred_element_type=F32)


def nt(a, b):
    return lax.dot_general(a, b, (((1,), (1,)), ((), ())), preferred_element_type=F32)


def tn(a, b):
    return lax.dot_general(a, b, (((0,), (0,)), ((), ())), preferred_element_type=F32)


def iota(shape, dim):
    return lax.broadcasted_iota(jnp.int32, shape, dim)


class Wires:
    def __init__(self, send, recv):
        self.send, self.recv = send, recv
        self.copies = {}
        self.sent = set()

    def start(self, key, src, dst, device):
        place = len(self.copies)
        copy = pltpu.make_async_remote_copy(
            src_ref=src,
            dst_ref=dst,
            send_sem=self.send.at[place],
            recv_sem=self.recv.at[place],
            device_id=device,
            device_id_type=MESH,
        )
        copy.start()
        self.copies[key] = copy

    def arrived(self, key):
        self.copies[key].wait_recv()

    def left(self, key):
        if key not in self.sent:
            self.sent.add(key)
            self.copies[key].wait_send()

    def finish(self):
        for key in self.copies:
            self.left(key)


N_COPIES = 56 + 7 + 3 + 4 + 48 + 20 + 20 + 48 + 56 + 30


def kernel(
    ids_ref, gates_ref, lat_ref, ctl_ref, og_ref, cs_ref, ng_ref, wi_ref, wo_ref,
    out_ref, sg_ref, gs_ref,
    zb, xst, xsl, rows, wi, wo, act, slope, fr, pb, own, part, codes, sel, gsel, pick, pick_t, meta, hid, gb,
    send, recv, lsem, free,
):
    me_s, me_e = lax.axis_index("seq"), lax.axis_index("expert")
    y, c = lax.div(me_s, 2), lax.rem(me_s, 2)
    z, x = lax.div(me_e, 4), lax.rem(me_e, 4)

    def z_at(delta):
        return (me_s, lax.rem(z + delta + 8, 8) * 4 + x)

    def x_at(delta):
        return (me_s, z * 4 + lax.rem(x + delta + 4, 4))

    odd = lax.rem(y, 2)
    sibling = (y * 2 + 1 - c, me_e)
    mates = {1: (lax.rem(y + 3 + 2 * odd, 4) * 2 + c, me_e), 2: ((y + 1 - 2 * odd) * 2 + c, me_e)}
    near = [
        (lax.rem(y + k // 4, 4) * 2 + c, z * 4 + lax.rem(x + k % 4, 4)) for k in range(1, 16)
    ]
    far = [
        (y * 2 + lax.rem(c + k % 2, 2), lax.rem(z + k // 2, 8) * 4 + x) for k in range(1, 16)
    ]
    peers = near + far

    barrier = pltpu.get_barrier_semaphore()
    for peer in peers:
        pl.semaphore_signal(barrier, inc=1, device_id=peer, device_id_type=MESH)

    local = []
    for k in range(2):
        local.append(
            pltpu.make_async_copy(
                wi_ref.at[0, :, pl.ds(256 * k, 256)], wi.at[:, pl.ds(SH * k, 256)], lsem.at[k]
            )
        )
        local.append(
            pltpu.make_async_copy(
                wo_ref.at[0, pl.ds(256 * k, 256)], wo.at[pl.ds(SH * k, 256)], lsem.at[2 + k]
            )
        )
    for copy in local:
        copy.start()

    scale, gain = cs_ref[...].reshape(1, D), ng_ref[...].reshape(1, D)
    hidden = lat_ref[...].astype(F32) + scale * ctl_ref[...].astype(F32)
    hid[...] = hidden
    inverse = 1.0 / jnp.sqrt(jnp.mean(hidden * hidden, axis=-1, keepdims=True) + 1e-06)
    zb[RES, 0:T] = (hidden * inverse * gain).astype(BF)
    zb[GRAD, 0:T] = og_ref[...]

    labels = iota((32, T), 0)
    hot0 = jnp.where(ids_ref[0:1] == labels, 1.0, 0.0)
    hot1 = jnp.where(ids_ref[1:2] == labels, 1.0, 0.0)
    before = jnp.where(iota((T, T), 0) < iota((T, T), 1), 1.0, 0.0).astype(BF)
    rank0 = jnp.sum(hot0 * nn(hot0.astype(BF), before), axis=0, keepdims=True)
    ahead = jnp.sum(hot0, axis=1, keepdims=True)
    rank1 = jnp.sum(hot1 * (nn(hot1.astype(BF), before) + ahead), axis=0, keepdims=True)
    line = iota((8, T), 0)
    mine = jnp.where(line == 0, ids_ref[0:1].astype(F32) * CAP + rank0, 0.0)
    mine = jnp.where(line == 1, ids_ref[1:2].astype(F32) * CAP + rank1, mine)
    mine = jnp.where(line == 2, gates_ref[0:1], mine)
    meta[0, 0:8] = jnp.where(line == 3, gates_ref[1:2], mine)

    pl.semaphore_wait(barrier, len(peers))
    wires = Wires(send, recv)

    def cols(q):
        return pl.ds(Q * q, Q)

    def z_own(u):
        a, q = u
        for h in range(2):
            for side in range(2):
                wires.start(
                    ("z", u, side, h),
                    zb.at[a, pl.ds(64 * h, 64), cols(q)],
                    zb.at[a, pl.ds(256 + T * side + 64 * h, 64), cols(q)],
                    z_at(1 - 2 * side),
                )

    def z_forward(u, d):
        a, q = u
        for h in range(2):
            for side in range(2):
                wires.arrived(("z", u, side, 2 * (d - 1) + h))
                src = zb.at[a, pl.ds(256 * d + T * side + 64 * h, 64), cols(q)]
                if d < 3:
                    dst = zb.at[a, pl.ds(256 * (d + 1) + T * side + 64 * h, 64), cols(q)]
                    wires.start(("z", u, side, 2 * d + h), src, dst, z_at(1 - 2 * side))
                elif side == h:
                    dst = zb.at[a, pl.ds(T + 64 * h, 64), cols(q)]
                    wires.start(("z", u, side, 6), src, dst, z_at(1 - 2 * side))

    def z_end(u):
        for side in range(2):
            wires.arrived(("z", u, side, 6))

    def z_left(u):
        for side in range(2):
            for m in range(7):
                wires.left(("z", u, side, m))

    def targets(g, k):
        return jnp.concatenate(
            [meta[0, pl.ds(16 * g + k, 1)], meta[0, pl.ds(16 * g + 8 + k, 1)]], axis=1
        )

    def prepare(g):
        first, second = codes[...] == targets(g, 0), codes[...] == targets(g, 1)
        sel[g] = jnp.where(first | second, 1.0, 0.0).astype(BF)

    def prepare_gates(g):
        first, second = codes[...] == targets(g, 0), codes[...] == targets(g, 1)
        gate = jnp.where(first, targets(g, 2), jnp.where(second, targets(g, 3), 0.0))
        high = gate.astype(BF)
        low = (gate - high.astype(F32)).astype(BF)
        eye = jnp.where(iota((192, 192), 0) == iota((192, 192), 1), 1.0, 0.0).astype(BF)
        gsel[g, 0] = tn(high, eye).astype(BF)
        gsel[g, 1] = tn(low, eye).astype(BF)

    def select(u, g):
        a, q = u
        got = nn(sel[g], zb[a, pl.ds(256 * g, 256), cols(q)]).astype(BF)
        xsl[a, pl.ds(PAIR * g, PAIR), cols(q)] = got[0:PAIR]
        xst[a, g, pl.ds(PAIR, 3 * PAIR), cols(q)] = got[PAIR:]
        for j in range(1, 4):
            wires.start(
                ("x", u, j, g),
                xst.at[a, g, pl.ds(PAIR * j, PAIR), cols(q)],
                xsl.at[a, pl.ds((4 * j + g) * PAIR, PAIR), cols(q)],
                x_at(j),
            )

    def block(o):
        return pl.ds(ROWS * o, ROWS)

    def compact(u):
        a, q = u
        for j in range(1, 4):
            for g in range(4):
                wires.left(("x", u, j, g))
            if q == 1:
                pl.semaphore_signal(free.at[a], inc=1, device_id=x_at(j), device_id_type=MESH)
        for g in (1, 2, 3, 0):
            for j in range(1, 4):
                wires.arrived(("x", u, j, g))
        rows[a, 0:ROWS, cols(q)] = nn(pick[...], xsl[a, :, cols(q)]).astype(BF)
        for k in (1, 2):
            wires.start(
                ("e", u, k), rows.at[a, block(0), cols(q)], rows.at[a, block(2 * k), cols(q)], mates[k]
            )
        wires.start(
            ("e", u, 0), rows.at[a, block(0), cols(q)], rows.at[a, block(1), cols(q)], sibling
        )

    def pass_rows(u):
        a, q = u
        for k in (1, 2):
            wires.arrived(("e", u, k))
            wires.start(
                ("e", u, 2 + k),
                rows.at[a, block(2 * k), cols(q)],
                rows.at[a, block(2 * k + 1), cols(q)],
                sibling,
            )

    def rows_here(a, k):
        for q in range(2):
            wires.arrived(("e", (a, q), 2 + k if k else 0))

    def forward(k):
        at, to, low, high = BLOCKS[k]
        rows_here(RES, k)

        @pl.loop(low // NT, high // NT)
        def _(i):
            tile = pl.ds(pl.multiple_of(i * NT, NT), NT)
            v = nn(rows[RES, pl.ds(at, 2 * ROWS)], wi[:, tile])
            inner = jnp.tanh(coeff * (v + cubic * v * v * v))
            act[pl.ds(to, 2 * ROWS), tile] = (0.5 * v * (1.0 + inner)).astype(BF)
            slope[pl.ds(to, 2 * ROWS), tile] = 0.5 * (1.0 + inner) + 0.5 * v * (
                1.0 - inner * inner
            ) * coeff * (1.0 + 3.0 * cubic * v * v)

    def backward(k):
        at, to, low, high = BLOCKS[k]
        rows_here(GRAD, k)

        @pl.loop(low // NT, high // NT)
        def _(i):
            tile = pl.ds(pl.multiple_of(i * NT, NT), NT)
            got = nt(rows[GRAD, pl.ds(at, 2 * ROWS)], wo[tile, :])
            act[pl.ds(to, 2 * ROWS), tile] = (got * slope[pl.ds(to, 2 * ROWS), tile]).astype(BF)

    def rows_left(a):
        for q in range(2):
            for k in range(5):
                wires.left(("e", (a, q), k))

    def result(q, k):
        at, to, low, high = BLOCKS[k]

        @pl.loop(0, Q // NT)
        def _(i):
            tile = pl.ds(pl.multiple_of(Q * q + i * NT, NT), NT)
            rows[RES, pl.ds(at, 2 * ROWS), tile] = nn(
                act[pl.ds(to, 2 * ROWS), low:high], wo[low:high, tile]
            ).astype(BF)

    def input_grad(q, k):
        at, to, low, high = BLOCKS[k]

        @pl.loop(0, Q // NT)
        def _(i):
            tile = pl.ds(pl.multiple_of(Q * q + i * NT, NT), NT)
            rows[GRAD, pl.ds(at, 2 * ROWS), tile] = nt(
                act[pl.ds(to, 2 * ROWS), low:high], wi[tile, low:high]
            ).astype(BF)

    def partial_sums(u, make):
        a, q = u
        for k in (1, 2, 0):
            make(q, k)
            wires.start(
                ("f", u, 2 + k if k else 0),
                rows.at[a, block(2 * k + 1), cols(q)],
                fr.at[a, 2 + k if k else 0, :, cols(q)],
                sibling,
            )

    def to_mates(u):
        a, q = u
        for k in (1, 2):
            wires.arrived(("f", u, 2 + k))
            rows[a, block(2 * k), cols(q)] = (
                rows[a, block(2 * k), cols(q)].astype(F32) + fr[a, 2 + k, :, cols(q)].astype(F32)
            ).astype(BF)
            wires.start(
                ("f", u, k), rows.at[a, block(2 * k), cols(q)], fr.at[a, k, :, cols(q)], mates[k]
            )

    def give_back(u):
        a, q = u
        for k in range(3):
            wires.arrived(("f", u, k))
        z_left(u)
        total = rows[a, block(0), cols(q)].astype(F32)
        for k in range(3):
            total = total + fr[a, k, :, cols(q)].astype(F32)
        zb[a, pl.ds(256, ROWS), cols(q)] = total.astype(BF)
        if q == 0:
            pl.semaphore_wait(free.at[a], 3)
        got = nn(pick_t[...], zb[a, pl.ds(256, ROWS), cols(q)]).astype(BF)
        for g in range(4):
            xst[a, g, 0:PAIR, cols(q)] = got[PAIR * g : PAIR * (g + 1)]
        xsl[a, pl.ds(4 * PAIR, 12 * PAIR), cols(q)] = got[4 * PAIR :]
        for g in (0, 3, 2, 1):
            for j in range(1, 4):
                wires.start(
                    ("r", u, j, g),
                    xsl.at[a, pl.ds((4 * j + g) * PAIR, PAIR), cols(q)],
                    xst.at[a, g, pl.ds(PAIR * j, PAIR), cols(q)],
                    x_at(-j),
                )

    def gathered(u, g):
        a, q = u
        for j in range(1, 4):
            wires.arrived(("r", u, j, g))
        got = xst[a, g, :, cols(q)]
        return nn(gsel[g, 0], got) + nn(gsel[g, 1], got)

    def z_back(u, side, m, src, g, h):
        a, q = u
        dst = pb.at[a, pl.ds(256 * g + T * side + 64 * h, 64), cols(q)]
        wires.start(("b", u, side, m), src, dst, z_at(2 * side - 1))

    def reduce_first(u):
        a, q = u
        got = gathered(u, 0)
        own[a, :, cols(q)] = got[0:T]
        zb[a, pl.ds(512, T), cols(q)] = got[T:].astype(BF)
        for side in range(2):
            z_back(u, side, 0, zb.at[a, pl.ds(512 + 64 * side, 64), cols(q)], 3, side)

    def reduce_next(u, g):
        a, q = u
        part[...] = gathered(u, g)
        order = ((0, 1), (1, 0), (0, 0), (1, 1)) if g == 3 else ((0, 0), (1, 0), (0, 1), (1, 1))
        for side, h in order:
            at = T * side + 64 * h
            value = part[at : at + 64]
            if g < 3 or side == h:
                wires.arrived(("b", u, side, 5 - 2 * g + h if g < 3 else 0))
                value = value + pb[a, pl.ds(256 * g + at, 64), cols(q)].astype(F32)
            pb[a, pl.ds(256 * g + at, 64), cols(q)] = value.astype(BF)
            src = pb.at[a, pl.ds(256 * g + at, 64), cols(q)]
            z_back(u, side, 7 - 2 * g + h, src, g - 1, h)

    def reduce_last(u):
        a, q = u
        for h in range(2):
            for side in range(2):
                wires.arrived(("b", u, side, 5 + h))
        return (
            own[a, :, cols(q)]
            + pb[a, 0:T, cols(q)].astype(F32)
            + pb[a, T:256, cols(q)].astype(F32)
        )

    r0, r1, g0, g1 = (RES, 0), (RES, 1), (GRAD, 0), (GRAD, 1)

    z_own(r0)
    for k in range(1, 8):
        wires.start(("mz", k), meta.at[0, pl.ds(0, 8)], meta.at[0, pl.ds(8 * Z_SLOT[k], 8)], z_at(k))
    for k, mate, to in ((0, 2, 256), (1, 1, 768)):
        wires.start(
            ("w", 0, k), wi_ref.at[0, :, pl.ds(256 * k, 256)], wi.at[:, pl.ds(to, 256)], mates[mate]
        )
    for k, mate, to in ((0, 2, 256), (1, 1, 768)):
        wires.start(
            ("w", 1, k), wo_ref.at[0, pl.ds(256 * k, 256)], wo.at[pl.ds(to, 256)], mates[mate]
        )
    spot = iota((PAIR, 256), 0)
    spot = jnp.where(spot >= CAP, spot - CAP + 1024, spot)
    spot = spot - jnp.where(iota((PAIR, 256), 1) >= T, 1024, 0)
    spot = jnp.where((spot >= 0) & (spot < CAP), spot, -65536).astype(F32)
    for j in range(4):
        first = (z * 4 + lax.rem(x + j, 4)) * CAP
        codes[pl.ds(PAIR * j, PAIR)] = spot + first.astype(F32)
    for k in range(1, 8):
        wires.arrived(("mz", k))
    for j in range(1, 4):
        wires.start(("mx", j), meta.at[0], meta.at[j], x_at(j))

    z_forward(r0, 1)
    z_own(r1)
    prepare(1)
    select(r0, 1)
    z_forward(r0, 2)
    prepare(2)
    select(r0, 2)
    z_forward(r1, 1)
    select(r1, 1)
    prepare(3)
    prepare(0)
    z_forward(r0, 3)
    select(r0, 3)

    for j in range(1, 4):
        wires.arrived(("mx", j))
    marks = meta[...].reshape(256, T)
    low = (me_e * CAP).astype(F32)
    named = (marks >= low) & (marks < low + CAP) & ((iota((256, T), 0) & 7) < 2)
    named = jnp.where(named, 1.0, 0.0).astype(BF)
    counts = nt(jnp.ones((8, T), BF), named).astype(BF)
    begin = (iota((256, N_SLOT), 0) >> 3) * CAP
    slot = iota((256, N_SLOT), 1)
    inside = (slot >= begin) & (slot < begin + CAP)
    filled = nn(counts, jnp.where(inside, 1.0, 0.0).astype(BF))
    offset = nn(counts, jnp.where(slot >= begin + CAP, 1.0, 0.0).astype(BF))
    slot = iota((8, N_SLOT), 1).astype(F32)
    rank = slot - CAP * jnp.floor((slot + 0.5) * (1.0 / CAP))
    place = jnp.where(rank < filled, offset + rank, -1.0)
    pick[...] = jnp.where(iota((ROWS, N_SLOT), 0).astype(F32) == place[0:1], 1.0, 0.0).astype(BF)

    z_forward(r1, 2)
    z_own(g0)
    select(r1, 2)
    z_end(r0)
    select(r0, 0)
    z_forward(r1, 3)
    select(r1, 3)
    compact(r0)
    z_forward(g0, 1)
    z_own(g1)
    select(g0, 1)
    z_end(r1)
    select(r1, 0)
    eye = jnp.where(iota((ROWS, ROWS), 0) == iota((ROWS, ROWS), 1), 1.0, 0.0).astype(BF)
    pick_t[...] = tn(pick[...], eye).astype(BF)
    prepare_gates(0)
    prepare_gates(1)
    z_forward(g0, 2)
    select(g0, 2)
    compact(r1)
    z_forward(g1, 1)
    select(g1, 1)
    for copy in local:
        copy.wait()
    for k in range(2):
        wires.arrived(("w", 0, k))
    forward(0)
    z_forward(g0, 3)
    select(g0, 3)
    prepare_gates(2)
    prepare_gates(3)
    z_forward(g1, 2)
    select(g1, 2)
    pass_rows(r0)
    z_end(g0)
    select(g0, 0)
    z_forward(g1, 3)
    select(g1, 3)
    compact(g0)
    pass_rows(r1)
    z_end(g1)
    select(g1, 0)
    forward(1)
    forward(2)
    for k in range(2):
        wires.arrived(("w", 1, k))
    rows_left(RES)
    partial_sums(r0, result)
    partial_sums(r1, result)
    to_mates(r0)
    compact(g1)
    to_mates(r1)
    pass_rows(g0)
    backward(0)
    give_back(r0)
    reduce_first(r0)
    pass_rows(g1)
    reduce_next(r0, 3)
    backward(1)
    backward(2)
    reduce_next(r0, 2)
    give_back(r1)
    rows_left(GRAD)
    partial_sums(g0, input_grad)
    reduce_next(r0, 1)
    to_mates(g0)
    partial_sums(g1, input_grad)
    reduce_first(r1)
    to_mates(g1)
    out_ref[:, cols(0)] = hid[:, cols(0)] + reduce_last(r0)
    reduce_next(r1, 3)
    reduce_next(r1, 2)
    give_back(g0)
    reduce_next(r1, 1)
    reduce_first(g0)
    give_back(g1)
    out_ref[:, cols(1)] = hid[:, cols(1)] + reduce_last(r1)
    reduce_next(g0, 3)
    reduce_first(g1)
    reduce_next(g0, 2)
    reduce_next(g1, 3)
    reduce_next(g0, 1)
    reduce_next(g1, 2)
    own[GRAD, :, cols(0)] = reduce_last(g0)
    reduce_next(g1, 1)
    own[GRAD, :, cols(1)] = reduce_last(g1)

    hidden = hid[...]
    inverse = 1.0 / jnp.sqrt(jnp.mean(hidden * hidden, axis=-1, keepdims=True) + 1e-06)
    normed = hidden * inverse
    normed_grad = own[GRAD] * gain
    mean = jnp.mean(normed_grad * normed, axis=-1, keepdims=True)
    sum_grad = inverse * (normed_grad - normed * mean) + og_ref[...].astype(F32)
    sg_ref[...] = sum_grad

    total = jnp.sum(sum_grad * ctl_ref[...].astype(F32), axis=0, keepdims=True)
    for base, here, others in ((0, y * 4 + x, near), (16, z * 2 + c, far)):
        gb[base + here] = total
        for k, other in enumerate(others):
            wires.start(("g", base, k), gb.at[base + here], gb.at[base + here], other)
        for k in range(len(others)):
            wires.arrived(("g", base, k))
        total = gb[base]
        for k in range(1, 16):
            total = total + gb[base + k]
    gs_ref[...] = total.reshape(D)
    wires.finish()


def body(
    latents, control, control_scale, norm_gain, expert_ids, gate_weights, expert_in, expert_out, out_grad
):
    vmem = pl.BlockSpec(memory_space=pltpu.VMEM)
    hbm = pl.BlockSpec(memory_space=pl.ANY)
    output, sum_grad, grad_scale = pl.pallas_call(
        kernel,
        out_shape=(
            jax.ShapeDtypeStruct((T, D), F32),
            jax.ShapeDtypeStruct((T, D), F32),
            jax.ShapeDtypeStruct((D,), F32),
        ),
        in_specs=[vmem] * 7 + [hbm] * 2,
        out_specs=(vmem,) * 3,
        scratch_shapes=[
            pltpu.VMEM((2, 4 * 256, D), BF),
            pltpu.VMEM((2, 4, 4 * PAIR, D), BF),
            pltpu.VMEM((2, N_SLOT, D), BF),
            pltpu.VMEM((2, 6 * ROWS, D), BF),
            pltpu.VMEM((D, HID), BF),
            pltpu.VMEM((HID, D), BF),
            pltpu.VMEM((4 * ROWS, HID), BF),
            pltpu.VMEM((4 * ROWS, HID), F32),
            pltpu.VMEM((2, 5, ROWS, D), BF),
            pltpu.VMEM((2, 4 * 256, D), BF),
            pltpu.VMEM((2, T, D), F32),
            pltpu.VMEM((256, Q), F32),
            pltpu.VMEM((4 * PAIR, 256), F32),
            pltpu.VMEM((4, 4 * PAIR, 256), BF),
            pltpu.VMEM((4, 2, 256, 4 * PAIR), BF),
            pltpu.VMEM((ROWS, N_SLOT), BF),
            pltpu.VMEM((N_SLOT, ROWS), BF),
            pltpu.VMEM((4, 64, T), F32),
            pltpu.VMEM((T, D), F32),
            pltpu.VMEM((32, 1, D), F32),
            pltpu.SemaphoreType.DMA((N_COPIES,)),
            pltpu.SemaphoreType.DMA((N_COPIES,)),
            pltpu.SemaphoreType.DMA((4,)),
            pltpu.SemaphoreType.REGULAR((2,)),
        ],
        compiler_params=pltpu.CompilerParams(
            collective_id=0, has_side_effects=True, vmem_limit_bytes=63 * 1024 * 1024
        ),
    )(
        expert_ids.T, gate_weights.T, latents, control, out_grad, control_scale, norm_gain,
        expert_in, expert_out,
    )
    return output.astype(BF), sum_grad.astype(BF), (sum_grad * control_scale).astype(BF), grad_scale


def solution(mesh):
    return jax.shard_map(
        body,
        mesh=mesh,
        in_specs=(
            P(("seq", "expert"), None),
            P(("seq", "expert"), None),
            P(),
            P(),
            P(("seq", "expert"), None),
            P(("seq", "expert"), None),
            P("expert", None, "seq"),
            P("expert", "seq", None),
            P(("seq", "expert"), None),
        ),
        out_specs=(
            P(("seq", "expert"), None),
            P(("seq", "expert"), None),
            P(("seq", "expert"), None),
            P(),
        ),
        check_vma=False,
    )
```

time: 233 us -> 204 us (0.88)
  Pallas kernels: 221 us -> 200 us
  local copies, waits for them, and re-layouts: 6.95 us -> 0.61 us
    pallas_call x1, Pallas kernels: 221 us -> 200 us  [body(): pl.pallas_call(kernel, out_shape=(jax.ShapeDtypeStruct((T, D), F32), jax....]
    unnamed x5 -> x7, local copies, waits for them, and re-layouts: 4.28 us -> 0.61 us
    broadcast_in_dim x3 -> x0, local copies, waits for them, and re-layouts: 2.59 us -> none  [the longest x1 1.3 us: body(): control_scale[None, :]]
where the time goes in v2:
time: 204 us
  Pallas kernels  200 us (98%)
  other arithmetic  2.93 us (1%)
    pallas_call x1, Pallas kernels, body(): pl.pallas_call(kernel, out_shape=(jax.ShapeDtypeStruct((T, D), F32), jax....  200 us

profile of v2, /device:TPU:1, one launch (start us, length us, event | category | flops | bytes accessed | tf_op | source)
XLA Modules:
  0.0 203.8 jit_solution(8463626508171516298)
XLA Ops:
  0.6 0.0 copy-start.1
  0.6 199.6 %shard_map.120 = (f32[128,1536]{1,0:T(8,128)}, f32[128,1536]{1,0:T(8,128)}, f32[1536]{0:T(1024)}) custom-call(s32[2,128]{1,0:T(2,128)} %bitcast.2, f32[2,128]{1,0:T(2,128)} %bitcast.3, bf16[128,1536]{1,0:T(8,128)(2,1)} %lat_ref.1, bf16[128,1536]{1,0:T(8,128)(2,1)} %ctl_ref.1, bf16[128,1536]{1,0:T(8,128)(2,1)} %og_ref.1, f32[1536]{0:T(1024)} %cs_ref.1, ...), custom_call_target="tpu_custom_call" | custom-call | tf_op jit(solution)/shard_map/pallas_call | solution.py:564
  200.3 0.0 copy-start
  200.3 0.0 copy-start.2
  200.3 2.0 convert_element_type.9
  202.3 0.0 copy-done.1
  202.3 0.0 copy-done
  202.3 0.9 multiply_convert_fusion
  203.2 0.0 copy-done.2
  203.2 0.6 copy.14
Async XLA Ops:
  0.6 201.7 %copy-start.1 = (f32[1536]{0:T(1024)S(1)}, f32[1536]{0:T(1024)}, u32[]{:S(2)}) copy-start(f32[1536]{0:T(1024)} %cs_ref.1) | copy-start | bytes 18436
  200.3 2.0 copy-start
  200.3 3.0 %copy-start.2 = (f32[1536]{0:T(1024)S(1)}, f32[1536]{0:T(1024)}, u32[]{:S(2)}) copy-start(f32[1536]{0:T(1024)} %get-tuple-element.19) | copy-start | bytes 18436

commit v3 on v2

--- a/solution.py
+++ b/solution.py
@@ -23,7 +23,6 @@
 NT = 256
 Q = D // 2
 N_SLOT = 32 * CAP
-BLOCKS = {0: (0, 0, 0, HID), 1: (2 * ROWS, 2 * ROWS, 0, SH), 2: (4 * ROWS, 2 * ROWS, SH, HID)}
 Z_SLOT = {1: 2, 2: 4, 3: 6, 4: 1, 5: 7, 6: 5, 7: 3}
 
 
@@ -75,13 +74,13 @@
             self.left(key)
 
 
-N_COPIES = 56 + 7 + 3 + 4 + 48 + 20 + 20 + 48 + 56 + 30
+N_COPIES = 56 + 7 + 3 + 3 + 48 + 12 + 12 + 48 + 56 + 30
 
 
 def kernel(
     ids_ref, gates_ref, lat_ref, ctl_ref, og_ref, cs_ref, ng_ref, wi_ref, wo_ref,
     out_ref, sg_ref, gs_ref,
-    zb, xst, xsl, rows, wi, wo, act, slope, fr, pb, own, part, codes, sel, gsel, pick, pick_t, meta, hid, gb,
+    zb, xst, xsl, rows, wi, wo, act, slope, fr, pb, own, part, codes, sel, gsel, pick, pick_t, meta, hid, inv, lat, ctl, gb,
     send, recv, lsem, free,
 ):
     me_s, me_e = lax.axis_index("seq"), lax.axis_index("expert")
@@ -96,7 +95,8 @@
 
     odd = lax.rem(y, 2)
     sibling = (y * 2 + 1 - c, me_e)
-    mates = {1: (lax.rem(y + 3 + 2 * odd, 4) * 2 + c, me_e), 2: ((y + 1 - 2 * odd) * 2 + c, me_e)}
+    row_mate = (lax.rem(y + 3 + 2 * odd, 4) * 2 + c, me_e)
+    weight_mate = ((y + 1 - 2 * odd) * 2 + c, me_e)
     near = [
         (lax.rem(y + k // 4, 4) * 2 + c, z * 4 + lax.rem(x + k % 4, 4)) for k in range(1, 16)
     ]
@@ -109,27 +109,26 @@
     for peer in peers:
         pl.semaphore_signal(barrier, inc=1, device_id=peer, device_id_type=MESH)
 
-    local = []
-    for k in range(2):
-        local.append(
-            pltpu.make_async_copy(
-                wi_ref.at[0, :, pl.ds(256 * k, 256)], wi.at[:, pl.ds(SH * k, 256)], lsem.at[k]
-            )
-        )
-        local.append(
-            pltpu.make_async_copy(
-                wo_ref.at[0, pl.ds(256 * k, 256)], wo.at[pl.ds(SH * k, 256)], lsem.at[2 + k]
-            )
-        )
-    for copy in local:
+    tokens = [
+        pltpu.make_async_copy(lat_ref, lat, lsem.at[2]),
+        pltpu.make_async_copy(ctl_ref, ctl, lsem.at[3]),
+        pltpu.make_async_copy(og_ref, zb.at[GRAD, pl.ds(0, T)], lsem.at[4]),
+    ]
+    local = [
+        pltpu.make_async_copy(wi_ref.at[0], wi.at[:, pl.ds(0, SH)], lsem.at[0]),
+        pltpu.make_async_copy(wo_ref.at[0], wo.at[pl.ds(0, SH)], lsem.at[1]),
+    ]
+    for copy in tokens + local:
         copy.start()
 
     scale, gain = cs_ref[...].reshape(1, D), ng_ref[...].reshape(1, D)
-    hidden = lat_ref[...].astype(F32) + scale * ctl_ref[...].astype(F32)
+    for load in tokens:
+        load.wait()
+    hidden = lat[...].astype(F32) + scale * ctl[...].astype(F32)
     hid[...] = hidden
     inverse = 1.0 / jnp.sqrt(jnp.mean(hidden * hidden, axis=-1, keepdims=True) + 1e-06)
     zb[RES, 0:T] = (hidden * inverse * gain).astype(BF)
-    zb[GRAD, 0:T] = og_ref[...]
+    inv[...] = inverse
 
     labels = iota((32, T), 0)
     hot0 = jnp.where(ids_ref[0:1] == labels, 1.0, 0.0)
@@ -228,107 +227,102 @@
             for j in range(1, 4):
                 wires.arrived(("x", u, j, g))
         rows[a, 0:ROWS, cols(q)] = nn(pick[...], xsl[a, :, cols(q)]).astype(BF)
-        for k in (1, 2):
-            wires.start(
-                ("e", u, k), rows.at[a, block(0), cols(q)], rows.at[a, block(2 * k), cols(q)], mates[k]
-            )
         wires.start(
             ("e", u, 0), rows.at[a, block(0), cols(q)], rows.at[a, block(1), cols(q)], sibling
         )
 
+    def rows_to_mate(u):
+        a, q = u
+        wires.start(
+            ("e", u, 1), rows.at[a, block(0), cols(q)], rows.at[a, block(2), cols(q)], row_mate
+        )
+
     def pass_rows(u):
         a, q = u
-        for k in (1, 2):
-            wires.arrived(("e", u, k))
-            wires.start(
-                ("e", u, 2 + k),
-                rows.at[a, block(2 * k), cols(q)],
-                rows.at[a, block(2 * k + 1), cols(q)],
-                sibling,
-            )
+        wires.arrived(("e", u, 1))
+        wires.start(
+            ("e", u, 2), rows.at[a, block(2), cols(q)], rows.at[a, block(3), cols(q)], sibling
+        )
 
     def rows_here(a, k):
         for q in range(2):
-            wires.arrived(("e", (a, q), 2 + k if k else 0))
+            wires.arrived(("e", (a, q), 2 * k))
 
     def forward(k):
-        at, to, low, high = BLOCKS[k]
+        here = pl.ds(2 * ROWS * k, 2 * ROWS)
         rows_here(RES, k)
 
-        @pl.loop(low // NT, high // NT)
+        @pl.loop(0, HID // NT)
         def _(i):
             tile = pl.ds(pl.multiple_of(i * NT, NT), NT)
-            v = nn(rows[RES, pl.ds(at, 2 * ROWS)], wi[:, tile])
+            v = nn(rows[RES, here], wi[:, tile])
             inner = jnp.tanh(coeff * (v + cubic * v * v * v))
-            act[pl.ds(to, 2 * ROWS), tile] = (0.5 * v * (1.0 + inner)).astype(BF)
-            slope[pl.ds(to, 2 * ROWS), tile] = 0.5 * (1.0 + inner) + 0.5 * v * (
+            act[here, tile] = (0.5 * v * (1.0 + inner)).astype(BF)
+            slope[here, tile] = 0.5 * (1.0 + inner) + 0.5 * v * (
                 1.0 - inner * inner
             ) * coeff * (1.0 + 3.0 * cubic * v * v)
 
     def backward(k):
-        at, to, low, high = BLOCKS[k]
+        here = pl.ds(2 * ROWS * k, 2 * ROWS)
         rows_here(GRAD, k)
 
-        @pl.loop(low // NT, high // NT)
+        @pl.loop(0, HID // NT)
         def _(i):
             tile = pl.ds(pl.multiple_of(i * NT, NT), NT)
-            got = nt(rows[GRAD, pl.ds(at, 2 * ROWS)], wo[tile, :])
-            act[pl.ds(to, 2 * ROWS), tile] = (got * slope[pl.ds(to, 2 * ROWS), tile]).astype(BF)
+            got = nt(rows[GRAD, here], wo[tile, :])
+            act[here, tile] = (got * slope[here, tile]).astype(BF)
 
     def rows_left(a):
         for q in range(2):
-            for k in range(5):
+            for k in range(3):
                 wires.left(("e", (a, q), k))
 
     def result(q, k):
-        at, to, low, high = BLOCKS[k]
+        here = pl.ds(2 * ROWS * k, 2 * ROWS)
 
         @pl.loop(0, Q // NT)
         def _(i):
             tile = pl.ds(pl.multiple_of(Q * q + i * NT, NT), NT)
-            rows[RES, pl.ds(at, 2 * ROWS), tile] = nn(
-                act[pl.ds(to, 2 * ROWS), low:high], wo[low:high, tile]
+            rows[RES, here, tile] = nn(
+                act[here, :], wo[:, tile]
             ).astype(BF)
 
     def input_grad(q, k):
-        at, to, low, high = BLOCKS[k]
+        here = pl.ds(2 * ROWS * k, 2 * ROWS)
 
         @pl.loop(0, Q // NT)
         def _(i):
             tile = pl.ds(pl.multiple_of(Q * q + i * NT, NT), NT)
-            rows[GRAD, pl.ds(at, 2 * ROWS), tile] = nt(
-                act[pl.ds(to, 2 * ROWS), low:high], wi[tile, low:high]
+            rows[GRAD, here, tile] = nt(
+                act[here, :], wi[tile, :]
             ).astype(BF)
 
     def partial_sums(u, make):
         a, q = u
-        for k in (1, 2, 0):
+        for k in (1, 0):
             make(q, k)
             wires.start(
-                ("f", u, 2 + k if k else 0),
+                ("f", u, 2 * k),
                 rows.at[a, block(2 * k + 1), cols(q)],
-                fr.at[a, 2 + k if k else 0, :, cols(q)],
+                fr.at[a, 2 * k, :, cols(q)],
                 sibling,
             )
 
-    def to_mates(u):
-        a, q = u
-        for k in (1, 2):
-            wires.arrived(("f", u, 2 + k))
-            rows[a, block(2 * k), cols(q)] = (
-                rows[a, block(2 * k), cols(q)].astype(F32) + fr[a, 2 + k, :, cols(q)].astype(F32)
-            ).astype(BF)
-            wires.start(
-                ("f", u, k), rows.at[a, block(2 * k), cols(q)], fr.at[a, k, :, cols(q)], mates[k]
-            )
+    def to_mate(u):
+        a, q = u
+        wires.arrived(("f", u, 2))
+        rows[a, block(2), cols(q)] = (
+            rows[a, block(2), cols(q)].astype(F32) + fr[a, 2, :, cols(q)].astype(F32)
+        ).astype(BF)
+        wires.start(("f", u, 1), rows.at[a, block(2), cols(q)], fr.at[a, 1, :, cols(q)], row_mate)
 
     def give_back(u):
         a, q = u
-        for k in range(3):
+        for k in range(2):
             wires.arrived(("f", u, k))
         z_left(u)
         total = rows[a, block(0), cols(q)].astype(F32)
-        for k in range(3):
+        for k in range(2):
             total = total + fr[a, k, :, cols(q)].astype(F32)
         zb[a, pl.ds(256, ROWS), cols(q)] = total.astype(BF)
         if q == 0:
@@ -337,14 +331,18 @@
         for g in range(4):
             xst[a, g, 0:PAIR, cols(q)] = got[PAIR * g : PAIR * (g + 1)]
         xsl[a, pl.ds(4 * PAIR, 12 * PAIR), cols(q)] = got[4 * PAIR :]
-        for g in (0, 3, 2, 1):
-            for j in range(1, 4):
-                wires.start(
-                    ("r", u, j, g),
-                    xsl.at[a, pl.ds((4 * j + g) * PAIR, PAIR), cols(q)],
-                    xst.at[a, g, pl.ds(PAIR * j, PAIR), cols(q)],
-                    x_at(-j),
-                )
+        slots_back(u, 0)
+        slots_back(u, 3)
+
+    def slots_back(u, g):
+        a, q = u
+        for j in range(1, 4):
+            wires.start(
+                ("r", u, j, g),
+                xsl.at[a, pl.ds((4 * j + g) * PAIR, PAIR), cols(q)],
+                xst.at[a, g, pl.ds(PAIR * j, PAIR), cols(q)],
+                x_at(-j),
+            )
 
     def gathered(u, g):
         a, q = u
@@ -361,6 +359,8 @@
     def reduce_first(u):
         a, q = u
         got = gathered(u, 0)
+        slots_back(u, 2)
+        slots_back(u, 1)
         own[a, :, cols(q)] = got[0:T]
         zb[a, pl.ds(512, T), cols(q)] = got[T:].astype(BF)
         for side in range(2):
@@ -396,14 +396,13 @@
     z_own(r0)
     for k in range(1, 8):
         wires.start(("mz", k), meta.at[0, pl.ds(0, 8)], meta.at[0, pl.ds(8 * Z_SLOT[k], 8)], z_at(k))
-    for k, mate, to in ((0, 2, 256), (1, 1, 768)):
+    wires.start(("w", 0), wi_ref.at[0], wi.at[:, pl.ds(SH, SH)], weight_mate)
+
+    def more_weights(q):
         wires.start(
-            ("w", 0, k), wi_ref.at[0, :, pl.ds(256 * k, 256)], wi.at[:, pl.ds(to, 256)], mates[mate]
+            ("w", 1 + q), wo_ref.at[0, :, cols(q)], wo.at[pl.ds(SH, SH), cols(q)], weight_mate
         )
-    for k, mate, to in ((0, 2, 256), (1, 1, 768)):
-        wires.start(
-            ("w", 1, k), wo_ref.at[0, pl.ds(256 * k, 256)], wo.at[pl.ds(to, 256)], mates[mate]
-        )
+
     spot = iota((PAIR, 256), 0)
     spot = jnp.where(spot >= CAP, spot - CAP + 1024, spot)
     spot = spot - jnp.where(iota((PAIR, 256), 1) >= T, 1024, 0)
@@ -454,7 +453,9 @@
     select(r0, 0)
     z_forward(r1, 3)
     select(r1, 3)
+    more_weights(0)
     compact(r0)
+    rows_to_mate(r0)
     z_forward(g0, 1)
     z_own(g1)
     select(g0, 1)
@@ -467,64 +468,65 @@
     z_forward(g0, 2)
     select(g0, 2)
     compact(r1)
+    rows_to_mate(r1)
     z_forward(g1, 1)
     select(g1, 1)
+    pass_rows(r0)
     for copy in local:
         copy.wait()
-    for k in range(2):
-        wires.arrived(("w", 0, k))
+    wires.arrived(("w", 0))
     forward(0)
     z_forward(g0, 3)
     select(g0, 3)
+    more_weights(1)
     prepare_gates(2)
     prepare_gates(3)
     z_forward(g1, 2)
     select(g1, 2)
-    pass_rows(r0)
+    pass_rows(r1)
     z_end(g0)
     select(g0, 0)
+    forward(1)
+    wires.arrived(("w", 1))
+    rows_left(RES)
+    partial_sums(r0, result)
     z_forward(g1, 3)
     select(g1, 3)
+    to_mate(r0)
     compact(g0)
-    pass_rows(r1)
+    rows_to_mate(g0)
     z_end(g1)
     select(g1, 0)
-    forward(1)
-    forward(2)
-    for k in range(2):
-        wires.arrived(("w", 1, k))
-    rows_left(RES)
-    partial_sums(r0, result)
+    wires.arrived(("w", 2))
     partial_sums(r1, result)
-    to_mates(r0)
     compact(g1)
-    to_mates(r1)
+    rows_to_mate(g1)
+    give_back(r0)
+    to_mate(r1)
     pass_rows(g0)
     backward(0)
-    give_back(r0)
     reduce_first(r0)
+    reduce_next(r0, 3)
     pass_rows(g1)
-    reduce_next(r0, 3)
     backward(1)
-    backward(2)
-    reduce_next(r0, 2)
-    give_back(r1)
     rows_left(GRAD)
     partial_sums(g0, input_grad)
+    give_back(r1)
+    reduce_next(r0, 2)
+    to_mate(g0)
+    partial_sums(g1, input_grad)
     reduce_next(r0, 1)
-    to_mates(g0)
-    partial_sums(g1, input_grad)
     reduce_first(r1)
-    to_mates(g1)
+    to_mate(g1)
     out_ref[:, cols(0)] = hid[:, cols(0)] + reduce_last(r0)
     reduce_next(r1, 3)
+    give_back(g0)
     reduce_next(r1, 2)
-    give_back(g0)
     reduce_next(r1, 1)
     reduce_first(g0)
     give_back(g1)
+    reduce_next(g0, 3)
     out_ref[:, cols(1)] = hid[:, cols(1)] + reduce_last(r1)
-    reduce_next(g0, 3)
     reduce_first(g1)
     reduce_next(g0, 2)
     reduce_next(g1, 3)
@@ -534,15 +536,14 @@
     reduce_next(g1, 1)
     own[GRAD, :, cols(1)] = reduce_last(g1)
 
-    hidden = hid[...]
-    inverse = 1.0 / jnp.sqrt(jnp.mean(hidden * hidden, axis=-1, keepdims=True) + 1e-06)
-    normed = hidden * inverse
+    inverse = inv[...]
+    normed = hid[...] * inverse
     normed_grad = own[GRAD] * gain
     mean = jnp.mean(normed_grad * normed, axis=-1, keepdims=True)
-    sum_grad = inverse * (normed_grad - normed * mean) + og_ref[...].astype(F32)
+    sum_grad = inverse * (normed_grad - normed * mean) + zb[GRAD, 0:T].astype(F32)
     sg_ref[...] = sum_grad
 
-    total = jnp.sum(sum_grad * ctl_ref[...].astype(F32), axis=0, keepdims=True)
+    total = jnp.sum(sum_grad * ctl[...].astype(F32), axis=0, keepdims=True)
     for base, here, others in ((0, y * 4 + x, near), (16, z * 2 + c, far)):
         gb[base + here] = total
         for k, other in enumerate(others):
@@ -568,18 +569,18 @@
             jax.ShapeDtypeStruct((T, D), F32),
             jax.ShapeDtypeStruct((D,), F32),
         ),
-        in_specs=[vmem] * 7 + [hbm] * 2,
+        in_specs=[vmem] * 2 + [hbm] * 3 + [vmem] * 2 + [hbm] * 2,
         out_specs=(vmem,) * 3,
         scratch_shapes=[
             pltpu.VMEM((2, 4 * 256, D), BF),
             pltpu.VMEM((2, 4, 4 * PAIR, D), BF),
             pltpu.VMEM((2, N_SLOT, D), BF),
-            pltpu.VMEM((2, 6 * ROWS, D), BF),
+            pltpu.VMEM((2, 4 * ROWS, D), BF),
             pltpu.VMEM((D, HID), BF),
             pltpu.VMEM((HID, D), BF),
             pltpu.VMEM((4 * ROWS, HID), BF),
             pltpu.VMEM((4 * ROWS, HID), F32),
-            pltpu.VMEM((2, 5, ROWS, D), BF),
+            pltpu.VMEM((2, 3, ROWS, D), BF),
             pltpu.VMEM((2, 4 * 256, D), BF),
             pltpu.VMEM((2, T, D), F32),
             pltpu.VMEM((256, Q), F32),
@@ -590,10 +591,13 @@
             pltpu.VMEM((N_SLOT, ROWS), BF),
             pltpu.VMEM((4, 64, T), F32),
             pltpu.VMEM((T, D), F32),
+            pltpu.VMEM((T, 1), F32),
+            pltpu.VMEM((T, D), BF),
+            pltpu.VMEM((T, D), BF),
             pltpu.VMEM((32, 1, D), F32),
             pltpu.SemaphoreType.DMA((N_COPIES,)),
             pltpu.SemaphoreType.DMA((N_COPIES,)),
-            pltpu.SemaphoreType.DMA((4,)),
+            pltpu.SemaphoreType.DMA((5,)),
             pltpu.SemaphoreType.REGULAR((2,)),
         ],
         compiler_params=pltpu.CompilerParams(

time: 204 us -> 196 us (0.961)
  Pallas kernels: 200 us -> 191 us
    pallas_call x1, Pallas kernels: 200 us -> 191 us  [body(): pl.pallas_call(kernel, out_shape=(jax.ShapeDtypeStruct((T, D), F32), jax....]
where the time goes in v3:
time: 196 us; the launch traced here: 195 us
  Pallas kernels  191 us (97%)
  other arithmetic  2.93 us (1%)
    pallas_call x1, Pallas kernels, body(): pl.pallas_call(kernel, out_shape=(jax.ShapeDtypeStruct((T, D), F32), jax....  191 us

profile of v3, /device:TPU:1, one launch (start us, length us, event | category | flops | bytes accessed | tf_op | source)
XLA Modules:
  0.0 195.4 jit_solution(9327070949266022086)
XLA Ops:
  0.6 0.0 copy-start.1
  0.6 191.2 %shard_map.120 = (f32[128,1536]{1,0:T(8,128)}, f32[128,1536]{1,0:T(8,128)}, f32[1536]{0:T(1024)}) custom-call(s32[2,128]{1,0:T(2,128)} %bitcast.2, f32[2,128]{1,0:T(2,128)} %bitcast.3, bf16[128,1536]{1,0:T(8,128)(2,1)} %lat_ref.1, bf16[128,1536]{1,0:T(8,128)(2,1)} %ctl_ref.1, bf16[128,1536]{1,0:T(8,128)(2,1)} %og_ref.1, f32[1536]{0:T(1024)} %cs_ref.1, ...), custom_call_target="tpu_custom_call" | custom-call | tf_op jit(solution)/shard_map/pallas_call | solution.py:565
  191.9 0.0 copy-start
  191.9 0.0 copy-start.2
  191.9 2.0 %convert_element_type.9 = bf16[128,1536]{1,0:T(8,128)(2,1)} convert(f32[128,1536]{1,0:T(8,128)} %get-tuple-element.7) | non-fusion elementwise | flops 196608 | bytes 1179648 | tf_op jit(solution)/shard_map/convert_element_type | solution.py:610
  193.9 0.0 copy-done.1
  193.9 0.0 copy-done
  193.9 0.9 multiply_convert_fusion
  194.8 0.0 copy-done.2
  194.8 0.6 copy.14
Async XLA Ops:
  0.6 193.2 %copy-start.1 = (f32[1536]{0:T(1024)S(1)}, f32[1536]{0:T(1024)}, u32[]{:S(2)}) copy-start(f32[1536]{0:T(1024)} %cs_ref.1) | copy-start | bytes 18436
  191.9 2.0 %copy-start = (f32[128,1536]{1,0:T(8,128)S(1)}, f32[128,1536]{1,0:T(8,128)}, u32[]{:S(2)}) copy-start(f32[128,1536]{1,0:T(8,128)} %get-tuple-element.8) | copy-start | bytes 2359300
  191.9 3.0 %copy-start.2 = (f32[1536]{0:T(1024)S(1)}, f32[1536]{0:T(1024)}, u32[]{:S(2)}) copy-start(f32[1536]{0:T(1024)} %get-tuple-element.19) | copy-start | bytes 18436

commit v4 on v3

--- a/solution.py
+++ b/solution.py
@@ -331,8 +331,8 @@
         for g in range(4):
             xst[a, g, 0:PAIR, cols(q)] = got[PAIR * g : PAIR * (g + 1)]
         xsl[a, pl.ds(4 * PAIR, 12 * PAIR), cols(q)] = got[4 * PAIR :]
-        slots_back(u, 0)
-        slots_back(u, 3)
+        for g in (0, 3, 2, 1):
+            slots_back(u, g)
 
     def slots_back(u, g):
         a, q = u
@@ -359,8 +359,6 @@
     def reduce_first(u):
         a, q = u
         got = gathered(u, 0)
-        slots_back(u, 2)
-        slots_back(u, 1)
         own[a, :, cols(q)] = got[0:T]
         zb[a, pl.ds(512, T), cols(q)] = got[T:].astype(BF)
         for side in range(2):
@@ -534,20 +532,24 @@
     reduce_next(g1, 2)
     own[GRAD, :, cols(0)] = reduce_last(g0)
     reduce_next(g1, 1)
-    own[GRAD, :, cols(1)] = reduce_last(g1)
 
     inverse = inv[...]
-    normed = hid[...] * inverse
-    normed_grad = own[GRAD] * gain
-    mean = jnp.mean(normed_grad * normed, axis=-1, keepdims=True)
-    sum_grad = inverse * (normed_grad - normed * mean) + zb[GRAD, 0:T].astype(F32)
-    sg_ref[...] = sum_grad
+    hid[...] = hid[...] * inverse
+    first = own[GRAD, :, cols(0)] * gain[:, 0:Q]
+    mean = jnp.sum(first * hid[:, cols(0)], axis=-1, keepdims=True)
+    own[GRAD, :, cols(0)] = inverse * first + zb[GRAD, 0:T, cols(0)].astype(F32)
+    second = reduce_last(g1) * gain[:, Q:D]
+    mean = (mean + jnp.sum(second * hid[:, cols(1)], axis=-1, keepdims=True)) * (1.0 / D)
+    own[GRAD, :, cols(1)] = inverse * second + zb[GRAD, 0:T, cols(1)].astype(F32)
+    sum_grad = own[GRAD] - hid[...] * (inverse * mean)
 
     total = jnp.sum(sum_grad * ctl[...].astype(F32), axis=0, keepdims=True)
     for base, here, others in ((0, y * 4 + x, near), (16, z * 2 + c, far)):
         gb[base + here] = total
         for k, other in enumerate(others):
             wires.start(("g", base, k), gb.at[base + here], gb.at[base + here], other)
+        if base == 0:
+            sg_ref[...] = sum_grad
         for k in range(len(others)):
             wires.arrived(("g", base, k))
         total = gb[base]

time: 196 us -> 195 us (level)
  no operation moved by 1% of the time
where the time goes in v4:
time: 195 us
  Pallas kernels  191 us (98%)
  other arithmetic  2.93 us (2%)
    pallas_call x1, Pallas kernels, body(): pl.pallas_call(kernel, out_shape=(jax.ShapeDtypeStruct((T, D), F32), jax....  191 us

profile of v4, /device:TPU:1, one launch (start us, length us, event | category | flops | bytes accessed | tf_op | source)
XLA Modules:
  0.0 195.0 jit_solution(12880382192884196336)
XLA Ops:
  0.6 0.0 copy-start.1
  0.6 190.8 %shard_map.120 = (f32[128,1536]{1,0:T(8,128)}, f32[128,1536]{1,0:T(8,128)}, f32[1536]{0:T(1024)}) custom-call(s32[2,128]{1,0:T(2,128)} %bitcast.2, f32[2,128]{1,0:T(2,128)} %bitcast.3, bf16[128,1536]{1,0:T(8,128)(2,1)} %lat_ref.1, bf16[128,1536]{1,0:T(8,128)(2,1)} %ctl_ref.1, bf16[128,1536]{1,0:T(8,128)(2,1)} %og_ref.1, f32[1536]{0:T(1024)} %cs_ref.1, ...), custom_call_target="tpu_custom_call" | custom-call | tf_op jit(solution)/shard_map/pallas_call | solution.py:567
  191.4 0.0 copy-start
  191.4 0.0 copy-start.2
  191.4 2.0 %convert_element_type.9 = bf16[128,1536]{1,0:T(8,128)(2,1)} convert(f32[128,1536]{1,0:T(8,128)} %get-tuple-element.7) | non-fusion elementwise | flops 196608 | bytes 1179648 | tf_op jit(solution)/shard_map/convert_element_type | solution.py:612
  193.4 0.0 copy-done.1
  193.4 0.0 copy-done
  193.4 0.9 multiply_convert_fusion
  194.4 0.0 copy-done.2
  194.4 0.6 copy.14
Async XLA Ops:
  0.6 192.8 %copy-start.1 = (f32[1536]{0:T(1024)S(1)}, f32[1536]{0:T(1024)}, u32[]{:S(2)}) copy-start(f32[1536]{0:T(1024)} %cs_ref.1) | copy-start | bytes 18436
  191.4 2.0 %copy-start = (f32[128,1536]{1,0:T(8,128)S(1)}, f32[128,1536]{1,0:T(8,128)}, u32[]{:S(2)}) copy-start(f32[128,1536]{1,0:T(8,128)} %get-tuple-element.8) | copy-start | bytes 2359300
  191.4 3.0 %copy-start.2 = (f32[1536]{0:T(1024)S(1)}, f32[1536]{0:T(1024)}, u32[]{:S(2)}) copy-start(f32[1536]{0:T(1024)} %get-tuple-element.19) | copy-start | bytes 18436
